TPU v7x, 768 devices: a whole 4x8x12 slice. The times are simulated.
768 devices in a mesh: row: 8 (over z_hi, core), col: 96 (over x, y, z_lo).
Axes of the slice: x: 4, y: 8, z: 12 (z_hi: 4, z_lo: 3; z = z_hi * 3 + z_lo), core: 2. Of those that a mesh axis runs over, the one named last changes fastest.
Arguments:
- features: bfloat16 [24576, 256], P(('row', 'col')), may hold values from -6 to 6
- weight: bfloat16 [256, 256], replicated, may hold values from -0.375 to 0.375
- out_counts: int32 [24576], P(('row', 'col')), may hold values from 32 to 256
- in_counts: int32 [24576], P(('col', 'row')), may hold values from 32 to 256
- tile_mask: int32 [96, 8, 36, 128, 128], P('col', 'row'), may hold values 0 or 1
- tile_pos: int32 [96, 8, 36], P('col', 'row'), may hold values from 0 to 47, as said below
- tile_count: int32 [96, 8], P('col', 'row'), may hold values from 1 to 36, as said below
- cotangent: bfloat16 [24576, 256], P(('col', 'row')), may hold values from -6 to 6
Outputs:
- output: bfloat16 [24576, 256], P(('col', 'row'))
- grad_features: bfloat16 [24576, 256], P(('row', 'col'))
- grad_weight: float32 [256, 256], replicated
Inputs may be any that keep to these rules, and one draw needn't show every extreme that they name: `tile_pos`: slots of one device name distinct positions. `tile_count`: some device has all 36 slots live.
All inputs are finite; a program needn't handle non-finite values. No bound on the sum of `tile_mask` on one device may be relied on, other than what follows from the above.
Results may differ from a plain program's by a relative error of at most 0.015.
Values may be sent and summed in bfloat16 or wider, within the bound.
No kernel may reach another device: no remote copies, remote signals or barrier semaphores. Data moves between devices by JAX's collectives and lax.ppermute only.
A program may use at most 32 MiB of HBM per device.

v0:
```python
import jax
import jax.numpy as jnp
from jax import lax
from jax.sharding import PartitionSpec as P


def forward_tiles(masks, places, number, gathered, tile_rows, tile_cols):
    width = gathered.shape[1]
    size = masks.shape[1]
    source_tiles = gathered.reshape(tile_cols, size, width)

    def forward_advance(index, total):
        place = places[index]
        block = masks[index].astype(jnp.bfloat16)
        source_piece = lax.dynamic_index_in_dim(source_tiles, place % tile_cols, 0, keepdims=False)
        return total.at[place // tile_cols].add(
            jnp.dot(block, source_piece, preferred_element_type=jnp.float32)
        )

    total = lax.fori_loop(
        0, number, forward_advance, jnp.zeros((tile_rows, size, width), jnp.float32)
    )
    return total.reshape(tile_rows * size, width)


def backward_tiles(masks, places, number, gathered, tile_rows, tile_cols):
    width = gathered.shape[1]
    size = masks.shape[1]
    target_tiles = gathered.reshape(tile_rows, size, width)

    def backward_advance(index, total):
        place = places[index]
        block = masks[index].astype(jnp.bfloat16)
        target_piece = lax.dynamic_index_in_dim(target_tiles, place // tile_cols, 0, keepdims=False)
        product = lax.dot_general(
            block, target_piece, (((0,), (0,)), ((), ())), preferred_element_type=jnp.float32
        )
        return total.at[place % tile_cols].add(product)

    total = lax.fori_loop(
        0, number, backward_advance, jnp.zeros((tile_cols, size, width), jnp.float32)
    )
    return total.reshape(tile_cols * size, width)


def local(features, weight, out_counts, in_counts, tile_mask, tile_pos, tile_count, cotangent):
    masks = tile_mask[0, 0]
    places = tile_pos[0, 0]
    number = tile_count[0, 0]
    size = masks.shape[1]
    node_rows = features.shape[0]
    tile_rows = node_rows * lax.axis_size("row") // size
    tile_cols = node_rows * lax.axis_size("col") // size
    out_scale = lax.rsqrt(out_counts.astype(jnp.float32))
    in_scale = lax.rsqrt(in_counts.astype(jnp.float32))
    source = (
        jnp.dot(features, weight, preferred_element_type=jnp.float32) * out_scale[:, None]
    ).astype(jnp.bfloat16)
    sources = lax.all_gather(source, "col", axis=0, tiled=True)
    forward = forward_tiles(masks, places, number, sources, tile_rows, tile_cols)
    forward_mine = lax.psum_scatter(forward, "row", scatter_dimension=0, tiled=True)
    output = (forward_mine * in_scale[:, None]).astype(jnp.bfloat16)
    scaled = (cotangent.astype(jnp.float32) * in_scale[:, None]).astype(jnp.bfloat16)
    targets = lax.all_gather(scaled, "row", axis=0, tiled=True)
    backward = backward_tiles(masks, places, number, targets, tile_rows, tile_cols)
    backward_mine = lax.psum_scatter(backward, "col", scatter_dimension=0, tiled=True)
    back_agg = (backward_mine * out_scale[:, None]).astype(jnp.bfloat16)
    grad_features = lax.dot_general(
        back_agg, weight, (((1,), (1,)), ((), ())), preferred_element_type=jnp.float32
    ).astype(jnp.bfloat16)
    partial_weight = lax.dot_general(
        features, back_agg, (((0,), (0,)), ((), ())), preferred_element_type=jnp.float32
    )
    grad_weight = lax.psum(partial_weight, ("row", "col"))
    return (output, grad_features, grad_weight)


def solution(mesh):
    placed = (
        P(("row", "col"), None),
        P(),
        P(("row", "col")),
        P(("col", "row")),
        P("col", "row", None, None, None),
        P("col", "row", None),
        P("col", "row"),
        P(("col", "row"), None),
    )
    return jax.shard_map(
        local,
        mesh=mesh,
        in_specs=placed,
        out_specs=(P(("col", "row"), None), P(("row", "col"), None), P()),
        check_vma=False,
    )
```

profile of v0, /device:TPU:6, one launch (start us, length us, event | category | flops | bytes accessed | tf_op | source)
XLA Modules:
  0.0 2108.7 jit_solution(9466266222589874453)
XLA Ops:
  9.6 454.5 %all-gather.2.cloned.1.call-done = bf16[3072,256]{1,0:T(8,128)(2,1)} async-done(((bf16[32,256]{1,0:T(8,128)(2,1)}), bf16[3072,256]{1,0:T(8,128)(2,1)}) %all-gather.2.cloned.1.call-update) | async-done | bytes 1572880 | tf_op jit(solution)/shard_map/all_gather | solution.py:59
  464.1 104.6 %while.26 = (s32[]{:T(128)}, f32[2,128,256]{2,1,0:T(8,128)S(1)}, s32[]{:T(128)}, s32[36]{0:T(128)}, s32[36,128,128]{2,1,0:T(8,128)}, /*index=5*/bf16[24,128,256]...) while((s32[]{:T(128)}, f32[2,128,256]{2,1,0:T(8,128)S(1)}, ...), condition=%wide.region_2.3_spmd, body=%wide.region_0.2_spmd.sunk | while | flops 8470568 | bytes 394655 | solution.py:20
  476.3 1.7 fusion.29
  490.2 1.7 fusion.29
  497.1 1.7 fusion.29
  510.9 1.7 fusion.29
  517.9 1.7 fusion.29
  524.8 1.7 fusion.29
  531.7 1.7 fusion.29
  538.7 1.7 fusion.29
  569.5 269.4 %reduce-scatter.3.cloned.1.call-done = f32[32,256]{1,0:T(8,128)} async-done(((f32[256,256]{1,0:T(8,128)}), f32[32,256]{1,0:T(8,128)}) %reduce-scatter.3.cloned.1.call-update) | async-done | bytes 32784 | tf_op jit(solution)/shard_map/reduce_scatter | solution.py:61
  840.4 16.4 all_gather.7
  857.1 86.7 %while.27 = (s32[]{:T(128)}, f32[24,128,256]{2,1,0:T(8,128)S(1)}, s32[]{:T(128)}, s32[36]{0:T(128)S(1)}, s32[36,128,128]{2,1,0:T(8,128)}, /*index=5*/bf16[2,128,...) while((s32[]{:T(128)}, f32[24,128,256]{2,1,0:T(8,128)S(1)}, ...), condition=%wide.region_6.7_spmd, body=%wide.region_4.6_spmd.sunk | while | flops 8470568 | bytes 394655 | solution.py:40
  861.1 1.7 fusion.32
  866.8 1.7 fusion.32
  872.6 1.7 fusion.32
  878.3 1.7 fusion.32
  884.1 1.7 fusion.32
  889.8 1.7 fusion.32
  895.5 1.7 fusion.32
  901.3 1.7 fusion.32
  907.0 1.7 fusion.32
  912.7 1.7 fusion.32
  918.5 1.7 fusion.32
  924.2 1.7 fusion.32
  930.0 1.7 fusion.32
  935.7 1.7 fusion.32
  941.4 1.7 fusion.32
  945.5 584.5 %reduce-scatter.5.cloned.1.call-done = f32[32,256]{1,0:T(8,128)} async-done(((f32[3072,256]{1,0:T(8,128)}), f32[32,256]{1,0:T(8,128)}) %reduce-scatter.5.cloned.1.call-update) | async-done | bytes 32784 | tf_op jit(solution)/shard_map/reduce_scatter | solution.py:66
  1530.0 1.7 convolution_bitcast_fusion.2
  1533.3 567.1 %all-reduce.2.cloned.1.call-done = f32[256,256]{0,1:T(8,128)} async-done(((f32[256,256]{0,1:T(8,128)}), f32[256,256]{0,1:T(8,128)}) %all-reduce.2.cloned.1.call-update) | async-done | bytes 262160 | tf_op jit(solution)/shard_map/psum | solution.py:74
  2100.4 1.8 copy.11
  (98 shorter events, 79.6 us)
Async XLA Ops:
  7.2 0.9 copy-start
  7.2 562.3 %copy-start.6 = (s32[32]{0:T(128)S(1)}, s32[32]{0:T(128)}, u32[]{:S(2)}) copy-start(s32[32]{0:T(128)} %param.19) | copy-start | bytes 388
  7.2 831.7 %copy-start.3 = (bf16[32,256]{1,0:T(8,128)(2,1)S(1)}, bf16[32,256]{1,0:T(8,128)(2,1)}, u32[]{:S(2)}) copy-start(bf16[32,256]{1,0:T(8,128)(2,1)} %param.23) | copy-start | bytes 49156
  7.2 456.9 %all-gather.2.cloned.1.call-start = ((), (), s32[]{:S(2)}) async-start(), calls=%async_computation.2 | async-start | bytes 1589248 | tf_op jit(solution)/shard_map/all_gather | solution.py:59
  9.6 829.4 %reduce-scatter.3.cloned.1.call-start = ((), (), s32[]{:S(2)}) async-start(), calls=%async_computation.3 | async-start | bytes 294912 | tf_op jit(solution)/shard_map/reduce_scatter | solution.py:61
  568.7 0.7 copy-start.2
  568.7 288.3 %copy-start.5 = (s32[3]{0:T(128)S(1)}, s32[3]{0:T(128)}, u32[]{:S(2)}) copy-start(s32[3]{0:T(128)} %constant.165.clone.1) | copy-start | bytes 40
  568.7 288.3 %copy-start.7 = (s32[36]{0:T(128)S(1)}, s32[36]{0:T(128)}, u32[]{:S(2)}) copy-start(s32[36]{0:T(128)} %get-tuple-element.413) | copy-start | bytes 436
  569.4 960.5 %reduce-scatter.5.cloned.1.call-start = ((), (), s32[]{:S(2)}) async-start(), calls=%async_computation.4 | async-start | bytes 3178496 | tf_op jit(solution)/shard_map/reduce_scatter | solution.py:66
  857.1 672.9 %copy-start.4 = (bf16[32,256]{1,0:T(8,128)(2,1)S(1)}, bf16[32,256]{1,0:T(8,128)(2,1)}, u32[]{:S(2)}) copy-start(bf16[32,256]{1,0:T(8,128)(2,1)} %param.16) | copy-start | bytes 49156
  943.8 1.6 copy-start.1
  945.5 1154.9 %all-reduce.2.cloned.1.call-start = ((), (), s32[]{:S(2)}) async-start(), calls=%async_computation.5 | async-start | bytes 524288 | tf_op jit(solution)/shard_map/psum | solution.py:74
Sparse Core Ops, SparseCore 0:
  11.0 453.0 all-gather.1
  569.6 269.3 reduce-scatter.2
  945.6 584.3 reduce-scatter.4
  1535.8 564.5 all-reduce.1
where the time goes:
time: 2090 us; the launch traced here: 2110 us
  waiting for transfers between devices  1880 us (90%)
  loops' own time  80.8 us (4%)
  matrix products  55.5 us (3%)
  other arithmetic  34.4 us (2%)
  local copies, waits for them, and re-layouts  32.1 us (2%)
    reduce_scatter x1, waiting for transfers between devices, local(): lax.psum_scatter(backward, 'col', scatter_dimension=0, tiled=True)  584 us
    psum x1, waiting for transfers between devices, local(): grad_weight = lax.psum(partial_weight, ('row', 'col'))  567 us
    all_gather x1, waiting for transfers between devices, local(): sources = lax.all_gather(source, 'col', axis=0, tiled=True)  454 us
    reduce_scatter x1, waiting for transfers between devices, local(): lax.psum_scatter(forward, 'row', scatter_dimension=0, tiled=True)  269 us
  transfers between devices with their start and end apart: 4, of which 4 were waited for; matrix products, arithmetic and copies ran while one was open for 0% of the time, Pallas kernels for 0%

commit v1 on v0

v1 whole, which is shorter than its diff:
```python
import jax
import jax.numpy as jnp
from jax import lax
from jax.experimental import pallas as pl
from jax.experimental.pallas import tpu as pltpu
from jax.sharding import Mesh, PartitionSpec as P

TILE = 128
STEP = 6
ROW = ("zh", "core")
COL = ("x", "y", "zl")
SIZES = {"zh": 4, "core": 2, "x": 4, "y": 8, "zl": 3}


def place_tiles(count_ref, place_ref, mask_ref, dense_ref):
    step = pl.program_id(0)
    tile_cols = dense_ref.shape[1] // TILE

    @pl.when(step == 0)
    def _():
        dense_ref[...] = jnp.zeros_like(dense_ref)

    for inner in range(STEP):
        slot = step * STEP + inner

        @pl.when(slot < count_ref[0])
        def _():
            place = place_ref[slot]
            row = pl.multiple_of(place // tile_cols * TILE, TILE)
            col = pl.multiple_of(place % tile_cols * TILE, TILE)
            block = mask_ref[inner].astype(jnp.float32).astype(jnp.bfloat16)
            dense_ref[pl.ds(row, TILE), pl.ds(col, TILE)] = block


def dense_block(masks, places, count, rows, cols):
    slots = masks.shape[0]
    return pl.pallas_call(
        place_tiles,
        out_shape=jax.ShapeDtypeStruct((rows, cols), jnp.bfloat16),
        grid_spec=pltpu.PrefetchScalarGridSpec(
            num_scalar_prefetch=2,
            grid=(slots // STEP,),
            in_specs=[pl.BlockSpec((STEP, TILE, TILE), lambda i, n, p: (i, 0, 0))],
            out_specs=pl.BlockSpec((rows, cols), lambda i, n, p: (0, 0)),
        ),
        compiler_params=pltpu.CompilerParams(vmem_limit_bytes=16 * 1024 * 1024),
        cost_estimate=pl.CostEstimate(
            flops=slots * TILE * TILE,
            bytes_accessed=slots * TILE * TILE * 4 + rows * cols * 2,
            transcendentals=0,
        ),
        name="place_tiles",
    )(count, places, masks)


def size_of(axes):
    size = 1
    for axis in axes:
        size *= SIZES[axis]
    return size


def spread(piece, axes):
    count = size_of(axes)
    return lax.all_to_all(jnp.broadcast_to(piece[None], (count, *piece.shape)), axes, 0, 0)


def swap(pieces, axes):
    return lax.all_to_all(pieces, axes, 0, 0)


def total(pieces):
    return jnp.sum(pieces.astype(jnp.float32), axis=0)


def shifted(piece, axis, step):
    size = SIZES[axis]
    return lax.ppermute(piece, axis, [(i, (i + step) % size) for i in range(size)])


def gather_by_shifts(piece, axis, dim):
    size, me = SIZES[axis], lax.axis_index(axis)
    shape = piece.shape[:dim] + (size,) + piece.shape[dim:]
    whole = jnp.zeros(shape, piece.dtype)
    for step in range(size):
        block = piece if step == 0 else shifted(piece, axis, step)
        whole = lax.dynamic_update_index_in_dim(whole, block, (me + size - step) % size, dim)
    return whole


def block_of(pieces, axis, step, dim):
    place = (lax.axis_index(axis) + step) % SIZES[axis]
    return lax.dynamic_index_in_dim(pieces, place, dim, keepdims=False)


def scatter_by_shifts(pieces, axis):
    whole = block_of(pieces, axis, 0, 0).astype(jnp.float32)
    for step in range(1, SIZES[axis]):
        block = shifted(block_of(pieces, axis, step, 0), axis, step)
        whole = whole + block.astype(jnp.float32)
    return whole.astype(pieces.dtype)


def beside(pieces, block):
    return jnp.concatenate(
        [pieces, jnp.broadcast_to(block[None], (pieces.shape[0], *block.shape))], axis=1
    )


def local(features, weight, out_counts, in_counts, tile_mask, tile_pos, tile_count, cotangent):
    bf16, f32 = jnp.bfloat16, jnp.float32
    mine, width = features.shape
    rows = mine * size_of(ROW)
    cols = mine * size_of(COL)
    out_scale = lax.rsqrt(out_counts.astype(f32))[:, None]
    in_scale = lax.rsqrt(in_counts.astype(f32))[:, None]
    scaled_features = (features.astype(f32) * out_scale).astype(bf16)
    scaled = (cotangent.astype(f32) * in_scale).astype(bf16)

    near = spread(scaled_features, ("y", "zl")).reshape(-1, width)
    across = gather_by_shifts(scaled, "zh", 0)
    near, across = lax.optimization_barrier((near, across))
    targets = gather_by_shifts(across, "core", 1).reshape(rows, width)
    dense = dense_block(tile_mask[0, 0], tile_pos[0, 0], tile_count[0], rows, cols)
    sources = spread(near, ("x",)).reshape(cols, width)

    backward = lax.dot_general(
        dense, targets, (((0,), (0,)), ((), ())), preferred_element_type=f32
    ).astype(bf16)
    thirds = backward.reshape(-1, SIZES["zl"], mine, width)
    kept, second, third = (block_of(thirds, "zl", step, 1) for step in range(3))

    forward = jnp.dot(dense, sources, preferred_element_type=f32).astype(bf16)
    outer = lax.dot_general(
        forward, targets, (((0,), (0,)), ((), ())), preferred_element_type=f32
    ).astype(bf16)
    outer = total(swap(outer.reshape(SIZES["y"], -1, width), ("y",))).astype(bf16)
    outer, second = lax.optimization_barrier((outer, shifted(second, "zl", 1)))
    outer = total(spread(outer, ("x", "zl"))).astype(bf16)
    outer, third = lax.optimization_barrier((outer, shifted(third, "zl", 2)))
    part = (kept.astype(f32) + second.astype(f32) + third.astype(f32)).astype(bf16)
    part = scatter_by_shifts(part.reshape(SIZES["x"], -1, mine, width), "x")
    both = total(swap(beside(forward.reshape(-1, mine, width), outer), ROW))
    forward_mine, outer = both[:mine], both[mine:].astype(bf16)
    output = (
        jnp.dot(forward_mine.astype(bf16), weight, preferred_element_type=f32) * in_scale
    ).astype(bf16)

    last = swap(beside(part, outer), ("y",))
    grad_weight = last[:, mine:].reshape(width, width).astype(f32)
    back_agg = (total(last[:, :mine]) * out_scale).astype(bf16)
    grad_features = lax.dot_general(
        back_agg, weight, (((1,), (1,)), ((), ())), preferred_element_type=f32
    ).astype(bf16)
    return (output, grad_features, grad_weight)


def solution(mesh):
    fine = Mesh(mesh.devices.reshape(tuple(SIZES.values())), tuple(SIZES))
    by_row, by_col = ROW + COL, COL + ROW
    placed = (
        P(by_row, None),
        P(),
        P(by_row),
        P(by_col),
        P(COL, ROW, None, None, None),
        P(COL, ROW, None),
        P(COL, ROW),
        P(by_col, None),
    )
    return jax.shard_map(
        local,
        mesh=fine,
        in_specs=placed,
        out_specs=(P(by_col, None), P(by_row, None), P()),
        check_vma=False,
    )
```

time: 2090 us -> 145 us (0.07)
  waiting for transfers between devices: 1880 us -> 34 us
  loops' own time: 80.8 us -> 0 us
  starting transfers between devices: 0.16 us -> 74.4 us
  matrix products: 55.5 us -> 4.38 us
  other arithmetic: 34.4 us -> 6.63 us
  local copies, waits for them, and re-layouts: 32.1 us -> 5.6 us
    reduce_scatter x2 -> x0, waiting for transfers between devices: 854 us -> none  [the longest x1 584 us: local(): lax.psum_scatter(backward, 'col', scatter_dimension=0, tiled=True)]
    psum x1 -> x0, waiting for transfers between devices: 567 us -> none  [local(): grad_weight = lax.psum(partial_weight, ('row', 'col'))]
    all_gather x1 -> x0, waiting for transfers between devices: 454 us -> none  [local(): sources = lax.all_gather(source, 'col', axis=0, tiled=True)]
    another operation x2 -> x0, loops' own time: 80.8 us -> none  [the longest x1 40.4 us: backward_tiles(): lax.fori_loop(0, number, backward_advance, jnp.zeros((tile_cols, size, wi...]
    dot_general x32 -> x4, matrix products: 54 us -> 3.58 us  [the longest x1 1.97 us: local(): forward = jnp.dot(dense, sources, preferred_element_type=f32).astype(bf16)]
    ppermute x0 -> x9, starting transfers between devices: none -> 41.8 us  [shifted(): lax.ppermute(piece, axis, [(i, (i + step) % size) for i in range(size)])]
    all_to_all x0 -> x5, starting transfers between devices: none -> 32.6 us  [the longest x3 22.2 us: spread(): lax.all_to_all(jnp.broadcast_to(piece[None], (count, *piece.shape)), axes...]
    another operation x30 -> x0, other arithmetic: 32.3 us -> none
  transfers between devices with their start and end apart: 4 -> 14, of which waited for: 4 -> 9; matrix products, arithmetic and copies ran while one was open for 0% -> 5% of each run, Pallas kernels for 0% -> 1%
where the time goes in v1:
time: 145 us; the launch traced here: 143 us
  starting transfers between devices  74.4 us (51%)
  waiting for transfers between devices  34 us (23%)
  blocking collectives  15.6 us (11%)
  other arithmetic  6.63 us (5%)
  local copies, waits for them, and re-layouts  5.6 us (4%)
  matrix products  4.38 us (3%)
  between operations  1.72 us (1%)
    ppermute x9, starting transfers between devices, shifted(): lax.ppermute(piece, axis, [(i, (i + step) % size) for i in range(size)])  41.8 us
    all_to_all x3, starting transfers between devices, spread(): lax.all_to_all(jnp.broadcast_to(piece[None], (count, *piece.shape)), axes...  22.2 us
    all_to_all x1, blocking collectives, swap(): return lax.all_to_all(pieces, axes, 0, 0)  15.6 us
    ppermute x9, waiting for transfers between devices, shifted(): lax.ppermute(piece, axis, [(i, (i + step) % size) for i in range(size)])  15.3 us
    all_to_all x2, waiting for transfers between devices, swap(): return lax.all_to_all(pieces, axes, 0, 0)  11.1 us
    all_to_all x2, starting transfers between devices, swap(): return lax.all_to_all(pieces, axes, 0, 0)  10.4 us
    all_to_all x3, waiting for transfers between devices, spread(): lax.all_to_all(jnp.broadcast_to(piece[None], (count, *piece.shape)), axes...  7.56 us
  transfers between devices with their start and end apart: 14, of which 9 were waited for; matrix products, arithmetic and copies ran while one was open for 5% of the time, Pallas kernels for 1%

profile of v1, /device:TPU:6, one launch (start us, length us, event | category | flops | bytes accessed | tf_op | source)
XLA Modules:
  0.0 143.5 jit_solution(15471982238957931222)
XLA Ops:
  2.9 11.0 %all-to-all-start = ((bf16[24,32,256]{2,1,0:T(8,128)(2,1)}), bf16[24,32,256]{2,1,0:T(8,128)(2,1)S(1)}, u32[]{:S(2)}, u32[]{:S(2)}) async-start(bf16[24,32,256]{2,1,0:T(8,128)(2,1)} %broadcast_in_dim.58), calls=%async_computation | async-start | bytes 786432 | tf_op jit(solution)/shard_map/all_to_all | solution.py:65
  14.6 0.8 bitcast_dynamic-update-slice_fusion.5
  15.4 9.1 %collective-permute-start = (bf16[32,256]{1,0:T(8,128)(2,1)S(1)}, bf16[32,256]{1,0:T(8,128)(2,1)S(1)}, u32[]{:S(2)}, u32[]{:S(2)}) collective-permute-start(bf16[32,256]{1,0:T(8,128)(2,1)S(1)} %get-tuple-element.16), channel_id=1, source_target_pairs={{0,192},{192,384},{384,576},{576,0},{1,193},{193,385},{385,577},{5... | collective-permute-start | bytes 49160 | tf_op jit(solution)/shard_map/ppermute | solution.py:78
  24.5 10.0 %collective-permute-start.1 = (bf16[32,256]{1,0:T(8,128)(2,1)S(1)}, bf16[32,256]{1,0:T(8,128)(2,1)S(1)}, u32[]{:S(2)}, u32[]{:S(2)}) collective-permute-start(bf16[32,256]{1,0:T(8,128)(2,1)S(1)} %get-tuple-element.16), channel_id=1, source_target_pairs={{0,384},{192,576},{384,0},{576,192},{1,385},{193,577},{385,1},{577... | collective-permute-start | bytes 49160 | tf_op jit(solution)/shard_map/ppermute | solution.py:78
  34.5 3.0 %collective-permute-start.2 = (bf16[32,256]{1,0:T(8,128)(2,1)S(1)}, bf16[32,256]{1,0:T(8,128)(2,1)S(1)}, u32[]{:S(2)}, u32[]{:S(2)}) collective-permute-start(bf16[32,256]{1,0:T(8,128)(2,1)S(1)} %get-tuple-element.16), channel_id=1, source_target_pairs={{0,576},{192,0},{384,192},{576,384},{1,577},{193,1},{385,193},{577... | collective-permute-start | bytes 49160 | tf_op jit(solution)/shard_map/ppermute | solution.py:78
  37.7 4.4 %collective-permute-done.2 = bf16[32,256]{1,0:T(8,128)(2,1)S(1)} collective-permute-done((bf16[32,256]{1,0:T(8,128)(2,1)S(1)}, bf16[32,256]{1,0:T(8,128)(2,1)S(1)}, u32[]{:S(2)}, u32[]{:S(2)}) %collective-permute-start.2) | collective-permute-done | bytes 16416 | tf_op jit(solution)/shard_map/ppermute | solution.py:78
  42.1 1.2 broadcast_in_dim.64
  43.3 4.9 %all-to-all-start.1 = ((bf16[4,768,256]{2,1,0:T(8,128)(2,1)}), bf16[4,768,256]{2,1,0:T(8,128)(2,1)}, u32[]{:S(2)}, u32[]{:S(2)}) async-start(bf16[4,768,256]{2,1,0:T(8,128)(2,1)} %broadcast_in_dim.64), calls=%async_computation.1 | async-start | bytes 3145728 | tf_op jit(solution)/shard_map/all_to_all | solution.py:65
  48.9 1.7 %copy-done.1 = s32[1,1,36,128,128]{4,3,2,1,0:T(8,128)S(1)} copy-done((s32[1,1,36,128,128]{4,3,2,1,0:T(8,128)S(1)}, s32[1,1,36,128,128]{4,3,2,1,0:T(8,128)}, u32[]{:S(2)}) %copy-start.1) | copy-done | bytes 2359320
  50.6 1.1 place_tiles.1
  51.6 1.9 %collective-permute-start.3 = (bf16[4,32,256]{2,1,0:T(8,128)(2,1)S(1)}, bf16[4,32,256]{2,1,0:T(8,128)(2,1)S(1)}, u32[]{:S(2)}, u32[]{:S(2)}) collective-permute-start(bf16[4,32,256]{2,1,0:T(8,128)(2,1)S(1)} %bitcast_dynamic-update-slice_fusion.2), channel_id=1, source_target_pairs={{0,96},{96,0},{1,97},{97,1},{2,98},{98,2},{3,99},{99,3},{4,100},{1... | collective-permute-start | bytes 196616 | tf_op jit(solution)/shard_map/ppermute | solution.py:78
  53.6 1.2 collective-permute-done.3
  55.4 1.1 dynamic-slice_bitcast_fusion
  56.5 4.3 %collective-permute-start.4 = (bf16[32,32,256]{2,1,0:T(8,128)(2,1)}, bf16[32,32,256]{2,1,0:T(8,128)(2,1)}, u32[]{:S(2)}, u32[]{:S(2)}) collective-permute-start(bf16[32,32,256]{2,1,0:T(8,128)(2,1)} %get-tuple-element.18), channel_id=1, source_target_pairs={{0,1},{1,2},{2,0},{3,4},{4,5},{5,3},{6,7},{7,8},{8,6},{9,10},{10,1... | collective-permute-start | bytes 1572872 | tf_op jit(solution)/shard_map/ppermute | solution.py:78
  60.8 4.4 %all-to-all-done.1 = bf16[4,768,256]{2,1,0:T(8,128)(2,1)} async-done(((bf16[4,768,256]{2,1,0:T(8,128)(2,1)}), bf16[4,768,256]{2,1,0:T(8,128)(2,1)}, u32[]{:S(2)}, u32[]{:S(2)}) %all-to-all-start.1) | async-done | bytes 1572896 | tf_op jit(solution)/shard_map/all_to_all | solution.py:65
  65.2 2.0 %convolution_convert_fusion.1 = bf16[256,256]{1,0:T(8,128)(2,1)S(1)} fusion(bf16[256,3072]{1,0:T(8,128)(2,1)S(1)} %place_tiles.1, bf16[3072,256]{1,0:T(8,128)(2,1)} %bitcast.8), kind=kOutput, calls=%fused_computation.1 | convolution fusion | flops 402718720 | bytes 3276800 | tf_op jit(solution)/shard_map/dot_general | solution.py:133
  67.4 15.6 %all_to_all.30 = bf16[8,32,256]{2,1,0:T(8,128)(2,1)S(1)} all-to-all(bf16[8,32,256]{2,1,0:T(8,128)(2,1)S(1)} %bitcast.61), channel_id=1, replica_groups=mesh['zh'=4,'core'=2,'x'=4,'y'=8,'zl'=3] {'y'}, dimensions={0} | all-to-all | bytes 262144 | tf_op jit(solution)/shard_map/all_to_all | solution.py:69
  83.7 6.3 %all-to-all-start.3 = ((bf16[12,32,256]{2,1,0:T(8,128)(2,1)}), bf16[12,32,256]{2,1,0:T(8,128)(2,1)S(1)}, u32[]{:S(2)}, u32[]{:S(2)}) async-start(bf16[12,32,256]{2,1,0:T(8,128)(2,1)} %broadcast_in_dim.68), calls=%async_computation.3 | async-start | bytes 393216 | tf_op jit(solution)/shard_map/all_to_all | solution.py:65
  90.1 4.3 %collective-permute-start.5 = (bf16[32,32,256]{2,1,0:T(8,128)(2,1)}, bf16[32,32,256]{2,1,0:T(8,128)(2,1)S(1)}, u32[]{:S(2)}, u32[]{:S(2)}) collective-permute-start(bf16[32,32,256]{2,1,0:T(8,128)(2,1)} %get-tuple-element.17), channel_id=1, source_target_pairs={{0,2},{1,0},{2,1},{3,5},{4,3},{5,4},{6,8},{7,6},{8,7},{9,11},{10,9... | collective-permute-start | bytes 1572872 | tf_op jit(solution)/shard_map/ppermute | solution.py:78
  94.4 3.2 %all-to-all-done.3 = bf16[12,32,256]{2,1,0:T(8,128)(2,1)S(1)} async-done(((bf16[12,32,256]{2,1,0:T(8,128)(2,1)}), bf16[12,32,256]{2,1,0:T(8,128)(2,1)S(1)}, u32[]{:S(2)}, u32[]{:S(2)}) %all-to-all-start.3) | async-done | bytes 196640 | tf_op jit(solution)/shard_map/all_to_all | solution.py:65
  97.6 4.4 %collective-permute-done.5 = bf16[32,32,256]{2,1,0:T(8,128)(2,1)S(1)} collective-permute-done((bf16[32,32,256]{2,1,0:T(8,128)(2,1)}, bf16[32,32,256]{2,1,0:T(8,128)(2,1)S(1)}, u32[]{:S(2)}, u32[]{:S(2)}) %collective-permute-start.5) | collective-permute-done | bytes 524320 | tf_op jit(solution)/shard_map/ppermute | solution.py:78
  102.8 7.0 %all-to-all-start.4 = ((bf16[8,64,256]{2,1,0:T(8,128)(2,1)}), bf16[8,64,256]{2,1,0:T(8,128)(2,1)S(1)}, u32[]{:S(2)}, u32[]{:S(2)}) async-start(bf16[8,64,256]{2,1,0:T(8,128)(2,1)} %pad_maximum_fusion), calls=%async_computation.4 | async-start | bytes 524288 | tf_op jit(solution)/shard_map/all_to_all | solution.py:69
  109.8 1.3 fusion.2
  111.1 2.0 %collective-permute-start.6 = (bf16[8,32,256]{2,1,0:T(8,128)(2,1)S(1)}, bf16[8,32,256]{2,1,0:T(8,128)(2,1)S(1)}, u32[]{:S(2)}, u32[]{:S(2)}) collective-permute-start(bf16[8,32,256]{2,1,0:T(8,128)(2,1)S(1)} %get-tuple-element.19), channel_id=1, source_target_pairs={{0,24},{24,48},{48,72},{72,0},{1,25},{25,49},{49,73},{73,1},{2,26}... | collective-permute-start | bytes 393224 | tf_op jit(solution)/shard_map/ppermute | solution.py:78
  113.1 3.9 %collective-permute-start.8 = (bf16[8,32,256]{2,1,0:T(8,128)(2,1)S(1)}, bf16[8,32,256]{2,1,0:T(8,128)(2,1)S(1)}, u32[]{:S(2)}, u32[]{:S(2)}) collective-permute-start(bf16[8,32,256]{2,1,0:T(8,128)(2,1)S(1)} %get-tuple-element.20), channel_id=1, source_target_pairs={{0,72},{24,0},{48,24},{72,48},{1,73},{25,1},{49,25},{73,49},{2,74}... | collective-permute-start | bytes 393224 | tf_op jit(solution)/shard_map/ppermute | solution.py:78
  117.0 3.4 %collective-permute-start.7 = (bf16[8,32,256]{2,1,0:T(8,128)(2,1)S(1)}, bf16[8,32,256]{2,1,0:T(8,128)(2,1)S(1)}, u32[]{:S(2)}, u32[]{:S(2)}) collective-permute-start(bf16[8,32,256]{2,1,0:T(8,128)(2,1)S(1)} %get-tuple-element.21), channel_id=1, source_target_pairs={{0,48},{24,72},{48,0},{72,24},{1,49},{25,73},{49,1},{73,25},{2,50}... | collective-permute-start | bytes 393224 | tf_op jit(solution)/shard_map/ppermute | solution.py:78
  120.4 1.7 %collective-permute-done.8 = bf16[8,32,256]{2,1,0:T(8,128)(2,1)S(1)} collective-permute-done((bf16[8,32,256]{2,1,0:T(8,128)(2,1)S(1)}, bf16[8,32,256]{2,1,0:T(8,128)(2,1)S(1)}, u32[]{:S(2)}, u32[]{:S(2)}) %collective-permute-start.8) | collective-permute-done | bytes 131104 | tf_op jit(solution)/shard_map/ppermute | solution.py:78
  122.1 3.7 %collective-permute-done.7 = bf16[8,32,256]{2,1,0:T(8,128)(2,1)S(1)} collective-permute-done((bf16[8,32,256]{2,1,0:T(8,128)(2,1)S(1)}, bf16[8,32,256]{2,1,0:T(8,128)(2,1)S(1)}, u32[]{:S(2)}, u32[]{:S(2)}) %collective-permute-start.7) | collective-permute-done | bytes 131104 | tf_op jit(solution)/shard_map/ppermute | solution.py:78
  125.8 1.5 %all-to-all-done.4 = bf16[8,64,256]{2,1,0:T(8,128)(2,1)S(1)} async-done(((bf16[8,64,256]{2,1,0:T(8,128)(2,1)}), bf16[8,64,256]{2,1,0:T(8,128)(2,1)S(1)}, u32[]{:S(2)}, u32[]{:S(2)}) %all-to-all-start.4) | async-done | bytes 262176 | tf_op jit(solution)/shard_map/all_to_all | solution.py:69
  128.1 3.4 %all-to-all-start.5 = ((bf16[8,64,256]{2,1,0:T(8,128)(2,1)}), bf16[8,64,256]{2,1,0:T(8,128)(2,1)S(1)}, u32[]{:S(2)}, u32[]{:S(2)}) async-start(bf16[8,64,256]{2,1,0:T(8,128)(2,1)} %pad_maximum_fusion.1), calls=%async_computation.5 | async-start | bytes 524288 | tf_op jit(solution)/shard_map/all_to_all | solution.py:69
  132.3 9.6 %all-to-all-done.5 = bf16[8,64,256]{2,1,0:T(8,128)(2,1)S(1)} async-done(((bf16[8,64,256]{2,1,0:T(8,128)(2,1)}), bf16[8,64,256]{2,1,0:T(8,128)(2,1)S(1)}, u32[]{:S(2)}, u32[]{:S(2)}) %all-to-all-start.5) | async-done | bytes 262176 | tf_op jit(solution)/shard_map/all_to_all | solution.py:69
  141.9 0.8 convolution_convert_fusion.3
  (38 shorter events, 7.8 us)
Async XLA Ops:
  0.6 130.9 %copy-start = (bf16[256,256]{1,0:T(8,128)(2,1)S(1)}, bf16[256,256]{1,0:T(8,128)(2,1)}, u32[]{:S(2)}) copy-start(bf16[256,256]{1,0:T(8,128)(2,1)} %param.9) | copy-start | bytes 393220
  2.9 39.2 %all-to-all-start = ((bf16[24,32,256]{2,1,0:T(8,128)(2,1)}), bf16[24,32,256]{2,1,0:T(8,128)(2,1)S(1)}, u32[]{:S(2)}, u32[]{:S(2)}) async-start(bf16[24,32,256]{2,1,0:T(8,128)(2,1)} %broadcast_in_dim.58), calls=%async_computation | async-start | bytes 786432 | tf_op jit(solution)/shard_map/all_to_all | solution.py:65
  15.4 22.2 %collective-permute-start = (bf16[32,256]{1,0:T(8,128)(2,1)S(1)}, bf16[32,256]{1,0:T(8,128)(2,1)S(1)}, u32[]{:S(2)}, u32[]{:S(2)}) collective-permute-start(bf16[32,256]{1,0:T(8,128)(2,1)S(1)} %get-tuple-element.16), channel_id=1, source_target_pairs={{0,192},{192,384},{384,576},{576,0},{1,193},{193,385},{385,577},{5... | collective-permute-start | bytes 49160 | tf_op jit(solution)/shard_map/ppermute | solution.py:78
  24.5 13.2 %collective-permute-start.1 = (bf16[32,256]{1,0:T(8,128)(2,1)S(1)}, bf16[32,256]{1,0:T(8,128)(2,1)S(1)}, u32[]{:S(2)}, u32[]{:S(2)}) collective-permute-start(bf16[32,256]{1,0:T(8,128)(2,1)S(1)} %get-tuple-element.16), channel_id=1, source_target_pairs={{0,384},{192,576},{384,0},{576,192},{1,385},{193,577},{385,1},{577... | collective-permute-start | bytes 49160 | tf_op jit(solution)/shard_map/ppermute | solution.py:78
  34.5 7.5 %collective-permute-start.2 = (bf16[32,256]{1,0:T(8,128)(2,1)S(1)}, bf16[32,256]{1,0:T(8,128)(2,1)S(1)}, u32[]{:S(2)}, u32[]{:S(2)}) collective-permute-start(bf16[32,256]{1,0:T(8,128)(2,1)S(1)} %get-tuple-element.16), channel_id=1, source_target_pairs={{0,576},{192,0},{384,192},{576,384},{1,577},{193,1},{385,193},{577... | collective-permute-start | bytes 49160 | tf_op jit(solution)/shard_map/ppermute | solution.py:78
  43.3 5.6 %copy-start.2 = (s32[1,1,36]{2,1,0:T(1,128)S(1)}, s32[1,1,36]{2,1,0:T(1,128)}, u32[]{:S(2)}) copy-start(s32[1,1,36]{2,1,0:T(1,128)} %param.13) | copy-start | bytes 436
  43.3 21.8 %all-to-all-start.1 = ((bf16[4,768,256]{2,1,0:T(8,128)(2,1)}), bf16[4,768,256]{2,1,0:T(8,128)(2,1)}, u32[]{:S(2)}, u32[]{:S(2)}) async-start(bf16[4,768,256]{2,1,0:T(8,128)(2,1)} %broadcast_in_dim.64), calls=%async_computation.1 | async-start | bytes 3145728 | tf_op jit(solution)/shard_map/all_to_all | solution.py:65
  48.9 1.7 %copy-start.1 = (s32[1,1,36,128,128]{4,3,2,1,0:T(8,128)S(1)}, s32[1,1,36,128,128]{4,3,2,1,0:T(8,128)}, u32[]{:S(2)}) copy-start(s32[1,1,36,128,128]{4,3,2,1,0:T(8,128)} %param.12) | copy-start | bytes 7077892
  51.6 3.1 %collective-permute-start.3 = (bf16[4,32,256]{2,1,0:T(8,128)(2,1)S(1)}, bf16[4,32,256]{2,1,0:T(8,128)(2,1)S(1)}, u32[]{:S(2)}, u32[]{:S(2)}) collective-permute-start(bf16[4,32,256]{2,1,0:T(8,128)(2,1)S(1)} %bitcast_dynamic-update-slice_fusion.2), channel_id=1, source_target_pairs={{0,96},{96,0},{1,97},{97,1},{2,98},{98,2},{3,99},{99,3},{4,100},{1... | collective-permute-start | bytes 196616 | tf_op jit(solution)/shard_map/ppermute | solution.py:78
  56.5 26.5 %collective-permute-start.4 = (bf16[32,32,256]{2,1,0:T(8,128)(2,1)}, bf16[32,32,256]{2,1,0:T(8,128)(2,1)}, u32[]{:S(2)}, u32[]{:S(2)}) collective-permute-start(bf16[32,32,256]{2,1,0:T(8,128)(2,1)} %get-tuple-element.18), channel_id=1, source_target_pairs={{0,1},{1,2},{2,0},{3,4},{4,5},{5,3},{6,7},{7,8},{8,6},{9,10},{10,1... | collective-permute-start | bytes 1572872 | tf_op jit(solution)/shard_map/ppermute | solution.py:78
  83.7 13.8 %all-to-all-start.3 = ((bf16[12,32,256]{2,1,0:T(8,128)(2,1)}), bf16[12,32,256]{2,1,0:T(8,128)(2,1)S(1)}, u32[]{:S(2)}, u32[]{:S(2)}) async-start(bf16[12,32,256]{2,1,0:T(8,128)(2,1)} %broadcast_in_dim.68), calls=%async_computation.3 | async-start | bytes 393216 | tf_op jit(solution)/shard_map/all_to_all | solution.py:65
  90.1 12.0 %collective-permute-start.5 = (bf16[32,32,256]{2,1,0:T(8,128)(2,1)}, bf16[32,32,256]{2,1,0:T(8,128)(2,1)S(1)}, u32[]{:S(2)}, u32[]{:S(2)}) collective-permute-start(bf16[32,32,256]{2,1,0:T(8,128)(2,1)} %get-tuple-element.17), channel_id=1, source_target_pairs={{0,2},{1,0},{2,1},{3,5},{4,3},{5,4},{6,8},{7,6},{8,7},{9,11},{10,9... | collective-permute-start | bytes 1572872 | tf_op jit(solution)/shard_map/ppermute | solution.py:78
  102.8 24.5 %all-to-all-start.4 = ((bf16[8,64,256]{2,1,0:T(8,128)(2,1)}), bf16[8,64,256]{2,1,0:T(8,128)(2,1)S(1)}, u32[]{:S(2)}, u32[]{:S(2)}) async-start(bf16[8,64,256]{2,1,0:T(8,128)(2,1)} %pad_maximum_fusion), calls=%async_computation.4 | async-start | bytes 524288 | tf_op jit(solution)/shard_map/all_to_all | solution.py:69
  111.1 9.3 %collective-permute-start.6 = (bf16[8,32,256]{2,1,0:T(8,128)(2,1)S(1)}, bf16[8,32,256]{2,1,0:T(8,128)(2,1)S(1)}, u32[]{:S(2)}, u32[]{:S(2)}) collective-permute-start(bf16[8,32,256]{2,1,0:T(8,128)(2,1)S(1)} %get-tuple-element.19), channel_id=1, source_target_pairs={{0,24},{24,48},{48,72},{72,0},{1,25},{25,49},{49,73},{73,1},{2,26}... | collective-permute-start | bytes 393224 | tf_op jit(solution)/shard_map/ppermute | solution.py:78
  113.1 9.0 %collective-permute-start.8 = (bf16[8,32,256]{2,1,0:T(8,128)(2,1)S(1)}, bf16[8,32,256]{2,1,0:T(8,128)(2,1)S(1)}, u32[]{:S(2)}, u32[]{:S(2)}) collective-permute-start(bf16[8,32,256]{2,1,0:T(8,128)(2,1)S(1)} %get-tuple-element.20), channel_id=1, source_target_pairs={{0,72},{24,0},{48,24},{72,48},{1,73},{25,1},{49,25},{73,49},{2,74}... | collective-permute-start | bytes 393224 | tf_op jit(solution)/shard_map/ppermute | solution.py:78
  117.0 8.7 %collective-permute-start.7 = (bf16[8,32,256]{2,1,0:T(8,128)(2,1)S(1)}, bf16[8,32,256]{2,1,0:T(8,128)(2,1)S(1)}, u32[]{:S(2)}, u32[]{:S(2)}) collective-permute-start(bf16[8,32,256]{2,1,0:T(8,128)(2,1)S(1)} %get-tuple-element.21), channel_id=1, source_target_pairs={{0,48},{24,72},{48,0},{72,24},{1,49},{25,73},{49,1},{73,25},{2,50}... | collective-permute-start | bytes 393224 | tf_op jit(solution)/shard_map/ppermute | solution.py:78
  128.1 13.8 %all-to-all-start.5 = ((bf16[8,64,256]{2,1,0:T(8,128)(2,1)}), bf16[8,64,256]{2,1,0:T(8,128)(2,1)S(1)}, u32[]{:S(2)}, u32[]{:S(2)}) async-start(bf16[8,64,256]{2,1,0:T(8,128)(2,1)} %pad_maximum_fusion.1), calls=%async_computation.5 | async-start | bytes 524288 | tf_op jit(solution)/shard_map/all_to_all | solution.py:69

commit v2 on v1

--- a/solution.py
+++ b/solution.py
@@ -30,6 +30,59 @@
             col = pl.multiple_of(place % tile_cols * TILE, TILE)
             block = mask_ref[inner].astype(jnp.float32).astype(jnp.bfloat16)
             dense_ref[pl.ds(row, TILE), pl.ds(col, TILE)] = block
+
+
+def scale_copies(count_ref, value_ref, copies_ref):
+    nodes = value_ref.shape[0]
+    scale = lax.rsqrt(count_ref[...].astype(jnp.float32))
+    here = lax.broadcasted_iota(jnp.int32, (nodes, nodes), 0)
+    there = lax.broadcasted_iota(jnp.int32, (nodes, nodes), 1)
+    scale = jnp.broadcast_to(scale, (nodes, nodes))
+    scale = jnp.sum(jnp.where(here == there, scale, 0.0), axis=1, keepdims=True)
+    scaled = (value_ref[...].astype(jnp.float32) * scale).astype(copies_ref.dtype)
+    for copy in range(copies_ref.shape[0]):
+        copies_ref[copy] = scaled
+
+
+def scaled_copies(values, counts, axes):
+    return pl.pallas_call(
+        scale_copies,
+        out_shape=jax.ShapeDtypeStruct((size_of(axes), *values.shape), values.dtype),
+        in_specs=[pl.BlockSpec(memory_space=pltpu.VMEM)] * 2,
+        out_specs=pl.BlockSpec(memory_space=pltpu.VMEM),
+        name="scale_copies",
+    )(counts.reshape(1, -1), values)
+
+
+def apply_dense(dense_ref, source_ref, target_ref, forward_ref, outer_ref):
+    turns, width = source_ref.shape[:2]
+    total = jnp.zeros(forward_ref.shape, jnp.float32)
+    for turn in range(turns):
+        total += jnp.dot(
+            dense_ref[:, turn * width : (turn + 1) * width],
+            source_ref[turn],
+            preferred_element_type=jnp.float32,
+        )
+    forward = total.astype(forward_ref.dtype)
+    forward_ref[...] = forward
+    outer_ref[...] = lax.dot_general(
+        forward, target_ref[...], (((0,), (0,)), ((), ())), preferred_element_type=jnp.float32
+    ).astype(outer_ref.dtype)
+
+
+def dense_products(dense, sources, targets):
+    rows, width = targets.shape
+    return pl.pallas_call(
+        apply_dense,
+        out_shape=(
+            jax.ShapeDtypeStruct((rows, width), jnp.bfloat16),
+            jax.ShapeDtypeStruct((width, width), jnp.bfloat16),
+        ),
+        in_specs=[pl.BlockSpec(memory_space=pltpu.VMEM)] * 3,
+        out_specs=[pl.BlockSpec(memory_space=pltpu.VMEM)] * 2,
+        compiler_params=pltpu.CompilerParams(vmem_limit_bytes=24 * 1024 * 1024),
+        name="apply_dense",
+    )(dense, sources, targets)
 
 
 def dense_block(masks, places, count, rows, cols):
@@ -60,9 +113,12 @@
     return size
 
 
+def copies_of(piece, axes):
+    return jnp.broadcast_to(piece[None], (size_of(axes), *piece.shape))
+
+
 def spread(piece, axes):
-    count = size_of(axes)
-    return lax.all_to_all(jnp.broadcast_to(piece[None], (count, *piece.shape)), axes, 0, 0)
+    return lax.all_to_all(copies_of(piece, axes), axes, 0, 0)
 
 
 def swap(pieces, axes):
@@ -78,12 +134,11 @@
     return lax.ppermute(piece, axis, [(i, (i + step) % size) for i in range(size)])
 
 
-def gather_by_shifts(piece, axis, dim):
+def in_order(blocks, axis, dim):
     size, me = SIZES[axis], lax.axis_index(axis)
-    shape = piece.shape[:dim] + (size,) + piece.shape[dim:]
-    whole = jnp.zeros(shape, piece.dtype)
-    for step in range(size):
-        block = piece if step == 0 else shifted(piece, axis, step)
+    shape = blocks[0].shape[:dim] + (size,) + blocks[0].shape[dim:]
+    whole = jnp.zeros(shape, blocks[0].dtype)
+    for step, block in enumerate(blocks):
         whole = lax.dynamic_update_index_in_dim(whole, block, (me + size - step) % size, dim)
     return whole
 
@@ -93,12 +148,11 @@
     return lax.dynamic_index_in_dim(pieces, place, dim, keepdims=False)
 
 
-def scatter_by_shifts(pieces, axis):
-    whole = block_of(pieces, axis, 0, 0).astype(jnp.float32)
-    for step in range(1, SIZES[axis]):
-        block = shifted(block_of(pieces, axis, step, 0), axis, step)
+def sum_of(blocks):
+    whole = blocks[0].astype(jnp.float32)
+    for block in blocks[1:]:
         whole = whole + block.astype(jnp.float32)
-    return whole.astype(pieces.dtype)
+    return whole.astype(blocks[0].dtype)
 
 
 def beside(pieces, block):
@@ -114,33 +168,36 @@
     cols = mine * size_of(COL)
     out_scale = lax.rsqrt(out_counts.astype(f32))[:, None]
     in_scale = lax.rsqrt(in_counts.astype(f32))[:, None]
-    scaled_features = (features.astype(f32) * out_scale).astype(bf16)
     scaled = (cotangent.astype(f32) * in_scale).astype(bf16)
 
-    near = spread(scaled_features, ("y", "zl")).reshape(-1, width)
-    across = gather_by_shifts(scaled, "zh", 0)
-    near, across = lax.optimization_barrier((near, across))
-    targets = gather_by_shifts(across, "core", 1).reshape(rows, width)
+    near = swap(scaled_copies(features, out_counts, ("y", "zl")), ("y", "zl"))
+    near = near.reshape(-1, width)
     dense = dense_block(tile_mask[0, 0], tile_pos[0, 0], tile_count[0], rows, cols)
-    sources = spread(near, ("x",)).reshape(cols, width)
+    across = in_order([scaled] + [shifted(scaled, "zh", step) for step in (1, 2, 3)], "zh", 0)
+    near, across, dense = lax.optimization_barrier((near, across, dense))
+    sources = spread(near, ("x",))
+    targets = in_order((across, shifted(across, "core", 1)), "core", 1).reshape(rows, width)
 
     backward = lax.dot_general(
         dense, targets, (((0,), (0,)), ((), ())), preferred_element_type=f32
     ).astype(bf16)
     thirds = backward.reshape(-1, SIZES["zl"], mine, width)
     kept, second, third = (block_of(thirds, "zl", step, 1) for step in range(3))
-
-    forward = jnp.dot(dense, sources, preferred_element_type=f32).astype(bf16)
-    outer = lax.dot_general(
-        forward, targets, (((0,), (0,)), ((), ())), preferred_element_type=f32
-    ).astype(bf16)
-    outer = total(swap(outer.reshape(SIZES["y"], -1, width), ("y",))).astype(bf16)
-    outer, second = lax.optimization_barrier((outer, shifted(second, "zl", 1)))
+    second, third = shifted(second, "zl", 1), shifted(third, "zl", 2)
+
+    forward, outer = dense_products(dense, sources, targets)
+    outer = copies_of(outer.reshape(SIZES["y"], -1, width), ("core",))
+    outer = total(swap(outer.reshape(-1, *outer.shape[2:]), ("core", "y"))).astype(bf16)
+    forward = forward.reshape(SIZES["zh"], SIZES["core"], mine, width)
+    other = shifted(block_of(forward, "core", 1, 1), "core", 1)
+    forward = sum_of((block_of(forward, "core", 0, 1), other))
+    outer, second, third, forward = lax.optimization_barrier((outer, second, third, forward))
+    part = sum_of((kept, second, third)).reshape(SIZES["x"], -1, mine, width)
+    kept, first, second, third = (block_of(part, "x", step, 0) for step in range(4))
     outer = total(spread(outer, ("x", "zl"))).astype(bf16)
-    outer, third = lax.optimization_barrier((outer, shifted(third, "zl", 2)))
-    part = (kept.astype(f32) + second.astype(f32) + third.astype(f32)).astype(bf16)
-    part = scatter_by_shifts(part.reshape(SIZES["x"], -1, mine, width), "x")
-    both = total(swap(beside(forward.reshape(-1, mine, width), outer), ROW))
+    outer, second = lax.optimization_barrier((outer, shifted(second, "x", 2)))
+    part = sum_of((kept, shifted(first, "x", 1), second, shifted(third, "x", 3)))
+    both = total(swap(beside(forward, outer), ("zh",)))
     forward_mine, outer = both[:mine], both[mine:].astype(bf16)
     output = (
         jnp.dot(forward_mine.astype(bf16), weight, preferred_element_type=f32) * in_scale

time: 145 us -> 139 us (0.959)
  blocking collectives: 15.6 us -> 0 us
  starting transfers between devices: 74.4 us -> 82.9 us
  Pallas kernels: 1.06 us -> 3.55 us
  matrix products: 4.38 us -> 2.18 us
  waiting for transfers between devices: 34 us -> 35.9 us
    all_to_all x2 -> x4, waiting for transfers between devices: 11.1 us -> 29 us  [swap(): return lax.all_to_all(pieces, axes, 0, 0)]
    all_to_all x1 -> x0, blocking collectives: 15.6 us -> none  [swap(): return lax.all_to_all(pieces, axes, 0, 0)]
    all_to_all x2 -> x4, starting transfers between devices: 10.4 us -> 25.8 us  [swap(): return lax.all_to_all(pieces, axes, 0, 0)]
    ppermute x9 -> x10, waiting for transfers between devices: 15.3 us -> 2.39 us  [shifted(): lax.ppermute(piece, axis, [(i, (i + step) % size) for i in range(size)])]
    all_to_all x3 -> x2, starting transfers between devices: 22.2 us -> 12.3 us  [spread(): return lax.all_to_all(copies_of(piece, axes), axes, 0, 0)]
    all_to_all x3 -> x2, waiting for transfers between devices: 7.56 us -> 4.45 us  [spread(): return lax.all_to_all(copies_of(piece, axes), axes, 0, 0)]
    ppermute x9 -> x10, starting transfers between devices: 41.8 us -> 44.8 us  [shifted(): lax.ppermute(piece, axis, [(i, (i + step) % size) for i in range(size)])]
    pallas_call x0 -> x2, Pallas kernels: none -> 2.47 us  [the longest x1 1.64 us: scaled_copies(): pl.pallas_call(scale_copies, out_shape=jax.ShapeDtypeStruct((size_of(axes...]
  transfers between devices with their start and end apart: 14 -> 16, of which waited for: 9 -> 7; matrix products, arithmetic and copies ran while one was open for 5% -> 5% of each run, Pallas kernels for 1% -> 1%
where the time goes in v2:
time: 139 us; the launch traced here: 138 us
  starting transfers between devices  82.9 us (60%)
  waiting for transfers between devices  35.9 us (26%)
  local copies, waits for them, and re-layouts  6.26 us (5%)
  other arithmetic  5.43 us (4%)
  Pallas kernels  3.55 us (3%)
  matrix products  2.18 us (2%)
  between operations  1.71 us (1%)
    ppermute x10, starting transfers between devices, shifted(): lax.ppermute(piece, axis, [(i, (i + step) % size) for i in range(size)])  44.8 us
    all_to_all x4, waiting for transfers between devices, swap(): return lax.all_to_all(pieces, axes, 0, 0)  29 us
    all_to_all x4, starting transfers between devices, swap(): return lax.all_to_all(pieces, axes, 0, 0)  25.8 us
    all_to_all x2, starting transfers between devices, spread(): return lax.all_to_all(copies_of(piece, axes), axes, 0, 0)  12.3 us
    all_to_all x2, waiting for transfers between devices, spread(): return lax.all_to_all(copies_of(piece, axes), axes, 0, 0)  4.45 us
  transfers between devices with their start and end apart: 16, of which 7 were waited for; matrix products, arithmetic and copies ran while one was open for 5% of the time, Pallas kernels for 1%

profile of v2, /device:TPU:6, one launch (start us, length us, event | category | flops | bytes accessed | tf_op | source)
XLA Modules:
  0.0 137.9 jit_solution(16030863939298402263)
XLA Ops:
  0.6 1.6 %scale_copies.1 = bf16[24,32,256]{2,1,0:T(8,128)(2,1)} custom-call(s32[1,32]{1,0:T(1,128)} %bitcast.66, bf16[32,256]{1,0:T(8,128)(2,1)} %value_ref.1), custom_call_target="tpu_custom_call" | custom-call | tf_op jit(solution)/shard_map/scale_copies/pallas_call | solution.py:48
  2.3 11.0 %all-to-all-start = ((bf16[24,32,256]{2,1,0:T(8,128)(2,1)}), bf16[24,32,256]{2,1,0:T(8,128)(2,1)S(1)}, u32[]{:S(2)}, u32[]{:S(2)}) async-start(bf16[24,32,256]{2,1,0:T(8,128)(2,1)} %scale_copies.1), calls=%async_computation | async-start | bytes 786432 | tf_op jit(solution)/shard_map/all_to_all | solution.py:125
  14.0 0.8 bitcast_dynamic-update-slice_fusion.5
  14.8 9.1 %collective-permute-start = (bf16[32,256]{1,0:T(8,128)(2,1)S(1)}, bf16[32,256]{1,0:T(8,128)(2,1)S(1)}, u32[]{:S(2)}, u32[]{:S(2)}) collective-permute-start(bf16[32,256]{1,0:T(8,128)(2,1)S(1)} %get-tuple-element.26), channel_id=1, source_target_pairs={{0,192},{192,384},{384,576},{576,0},{1,193},{193,385},{385,577},{5... | collective-permute-start | bytes 49160 | tf_op jit(solution)/shard_map/ppermute | solution.py:134
  23.9 10.0 %collective-permute-start.1 = (bf16[32,256]{1,0:T(8,128)(2,1)S(1)}, bf16[32,256]{1,0:T(8,128)(2,1)S(1)}, u32[]{:S(2)}, u32[]{:S(2)}) collective-permute-start(bf16[32,256]{1,0:T(8,128)(2,1)S(1)} %get-tuple-element.26), channel_id=1, source_target_pairs={{0,384},{192,576},{384,0},{576,192},{1,385},{193,577},{385,1},{577... | collective-permute-start | bytes 49160 | tf_op jit(solution)/shard_map/ppermute | solution.py:134
  33.9 3.0 %collective-permute-start.2 = (bf16[32,256]{1,0:T(8,128)(2,1)S(1)}, bf16[32,256]{1,0:T(8,128)(2,1)S(1)}, u32[]{:S(2)}, u32[]{:S(2)}) collective-permute-start(bf16[32,256]{1,0:T(8,128)(2,1)S(1)} %get-tuple-element.26), channel_id=1, source_target_pairs={{0,576},{192,0},{384,192},{576,384},{1,577},{193,1},{385,193},{577... | collective-permute-start | bytes 49160 | tf_op jit(solution)/shard_map/ppermute | solution.py:134
  37.7 1.7 %copy-done.1 = s32[1,1,36,128,128]{4,3,2,1,0:T(8,128)S(1)} copy-done((s32[1,1,36,128,128]{4,3,2,1,0:T(8,128)S(1)}, s32[1,1,36,128,128]{4,3,2,1,0:T(8,128)}, u32[]{:S(2)}) %copy-start.1) | copy-done | bytes 2359320
  40.0 1.1 place_tiles.1.dense_ref
  41.4 1.2 broadcast_in_dim.64
  42.7 4.8 %all-to-all-start.1 = ((bf16[4,768,256]{2,1,0:T(8,128)(2,1)}), bf16[4,768,256]{2,1,0:T(8,128)(2,1)S(1)}, u32[]{:S(2)}, u32[]{:S(2)}) async-start(bf16[4,768,256]{2,1,0:T(8,128)(2,1)} %broadcast_in_dim.64), calls=%async_computation.1 | async-start | bytes 3145728 | tf_op jit(solution)/shard_map/all_to_all | solution.py:121
  47.4 1.9 %collective-permute-start.3 = (bf16[4,32,256]{2,1,0:T(8,128)(2,1)S(1)}, bf16[4,32,256]{2,1,0:T(8,128)(2,1)S(1)}, u32[]{:S(2)}, u32[]{:S(2)}) collective-permute-start(bf16[4,32,256]{2,1,0:T(8,128)(2,1)S(1)} %bitcast_dynamic-update-slice_fusion.2), channel_id=1, source_target_pairs={{0,96},{96,0},{1,97},{97,1},{2,98},{98,2},{3,99},{99,3},{4,100},{1... | collective-permute-start | bytes 196616 | tf_op jit(solution)/shard_map/ppermute | solution.py:134
  49.4 1.2 collective-permute-done.3
  51.2 1.1 dynamic-slice_bitcast_fusion
  52.4 4.2 %collective-permute-start.4 = (bf16[32,32,256]{2,1,0:T(8,128)(2,1)}, bf16[32,32,256]{2,1,0:T(8,128)(2,1)}, u32[]{:S(2)}, u32[]{:S(2)}) collective-permute-start(bf16[32,32,256]{2,1,0:T(8,128)(2,1)} %get-tuple-element.28), channel_id=1, source_target_pairs={{0,1},{1,2},{2,0},{3,4},{4,5},{5,3},{6,7},{7,8},{8,6},{9,10},{10,1... | collective-permute-start | bytes 1572872 | tf_op jit(solution)/shard_map/ppermute | solution.py:134
  56.6 3.7 %collective-permute-start.5 = (bf16[32,32,256]{2,1,0:T(8,128)(2,1)}, bf16[32,32,256]{2,1,0:T(8,128)(2,1)}, u32[]{:S(2)}, u32[]{:S(2)}) collective-permute-start(bf16[32,32,256]{2,1,0:T(8,128)(2,1)} %get-tuple-element.27), channel_id=1, source_target_pairs={{0,2},{1,0},{2,1},{3,5},{4,3},{5,4},{6,8},{7,6},{8,7},{9,11},{10,9... | collective-permute-start | bytes 1572872 | tf_op jit(solution)/shard_map/ppermute | solution.py:134
  60.3 4.4 %all-to-all-done.1.source_ref = bf16[4,768,256]{2,1,0:T(8,128)(2,1)S(1)} async-done(((bf16[4,768,256]{2,1,0:T(8,128)(2,1)}), bf16[4,768,256]{2,1,0:T(8,128)(2,1)S(1)}, u32[]{:S(2)}, u32[]{:S(2)}) %all-to-all-start.1) | async-done | bytes 1572896 | tf_op jit(solution)/shard_map/all_to_all | solution.py:121
  64.8 0.8 apply_dense.1
  66.3 7.0 %all-to-all-start.2 = ((bf16[16,32,256]{2,1,0:T(8,128)(2,1)}), bf16[16,32,256]{2,1,0:T(8,128)(2,1)S(1)}, u32[]{:S(2)}, u32[]{:S(2)}) async-start(bf16[16,32,256]{2,1,0:T(8,128)(2,1)} %bitcast.14), calls=%async_computation.2 | async-start | bytes 524288 | tf_op jit(solution)/shard_map/all_to_all | solution.py:125
  73.4 2.3 %collective-permute-start.6 = (bf16[4,32,256]{2,1,0:T(8,128)(2,1)S(1)}, bf16[4,32,256]{2,1,0:T(8,128)(2,1)S(1)}, u32[]{:S(2)}, u32[]{:S(2)}) collective-permute-start(bf16[4,32,256]{2,1,0:T(8,128)(2,1)S(1)} %dynamic-slice_bitcast_fusion.5), channel_id=1, source_target_pairs={{0,96},{96,0},{1,97},{97,1},{2,98},{98,2},{3,99},{99,3},{4,100},{1... | collective-permute-start | bytes 196616 | tf_op jit(solution)/shard_map/ppermute | solution.py:134
  75.7 0.9 collective-permute-done.6
  76.6 7.2 %all-to-all-done.2 = bf16[16,32,256]{2,1,0:T(8,128)(2,1)S(1)} async-done(((bf16[16,32,256]{2,1,0:T(8,128)(2,1)}), bf16[16,32,256]{2,1,0:T(8,128)(2,1)S(1)}, u32[]{:S(2)}, u32[]{:S(2)}) %all-to-all-start.2) | async-done | bytes 262176 | tf_op jit(solution)/shard_map/all_to_all | solution.py:125
  84.5 7.6 %all-to-all-start.3 = ((bf16[12,32,256]{2,1,0:T(8,128)(2,1)}), bf16[12,32,256]{2,1,0:T(8,128)(2,1)S(1)}, u32[]{:S(2)}, u32[]{:S(2)}) async-start(bf16[12,32,256]{2,1,0:T(8,128)(2,1)} %broadcast_in_dim.70), calls=%async_computation.3 | async-start | bytes 393216 | tf_op jit(solution)/shard_map/all_to_all | solution.py:121
  92.1 1.6 %fusion.2 = bf16[32,32,256]{2,1,0:T(8,128)(2,1)S(1)} fusion(bf16[32,32,256]{2,1,0:T(8,128)(2,1)} %collective-permute-done.5, bf16[32,32,256]{2,1,0:T(8,128)(2,1)} %collective-permute-done.4, bf16[32,3,32,256]{3,2,1,0:T(8,128)(2,1)} %bitcast.62, s32[]{:T(128)S(6)} %select_n.128), kind=kLoop, calls=%fused_computation.6 | loop fusion | flops 1572864 | bytes 2097156 | tf_op jit(solution)/shard_map/convert_element_type | solution.py:155
  93.8 3.4 %collective-permute-start.7 = (bf16[8,32,256]{2,1,0:T(8,128)(2,1)S(1)}, bf16[8,32,256]{2,1,0:T(8,128)(2,1)S(1)}, u32[]{:S(2)}, u32[]{:S(2)}) collective-permute-start(bf16[8,32,256]{2,1,0:T(8,128)(2,1)S(1)} %get-tuple-element.31), channel_id=1, source_target_pairs={{0,48},{24,72},{48,0},{72,24},{1,49},{25,73},{49,1},{73,25},{2,50}... | collective-permute-start | bytes 393224 | tf_op jit(solution)/shard_map/ppermute | solution.py:134
  97.2 1.9 %collective-permute-start.9 = (bf16[8,32,256]{2,1,0:T(8,128)(2,1)S(1)}, bf16[8,32,256]{2,1,0:T(8,128)(2,1)S(1)}, u32[]{:S(2)}, u32[]{:S(2)}) collective-permute-start(bf16[8,32,256]{2,1,0:T(8,128)(2,1)S(1)} %get-tuple-element.30), channel_id=1, source_target_pairs={{0,72},{24,0},{48,24},{72,48},{1,73},{25,1},{49,25},{73,49},{2,74}... | collective-permute-start | bytes 393224 | tf_op jit(solution)/shard_map/ppermute | solution.py:134
  99.1 5.1 %collective-permute-start.8 = (bf16[8,32,256]{2,1,0:T(8,128)(2,1)S(1)}, bf16[8,32,256]{2,1,0:T(8,128)(2,1)S(1)}, u32[]{:S(2)}, u32[]{:S(2)}) collective-permute-start(bf16[8,32,256]{2,1,0:T(8,128)(2,1)S(1)} %get-tuple-element.29), channel_id=1, source_target_pairs={{0,24},{24,48},{48,72},{72,0},{1,25},{25,49},{49,73},{73,1},{2,26}... | collective-permute-start | bytes 393224 | tf_op jit(solution)/shard_map/ppermute | solution.py:134
  105.0 3.9 %all-to-all-start.4 = ((bf16[4,64,256]{2,1,0:T(8,128)(2,1)}), bf16[4,64,256]{2,1,0:T(8,128)(2,1)S(1)}, u32[]{:S(2)}, u32[]{:S(2)}) async-start(bf16[4,64,256]{2,1,0:T(8,128)(2,1)} %pad_maximum_fusion.1), calls=%async_computation.4 | async-start | bytes 262144 | tf_op jit(solution)/shard_map/all_to_all | solution.py:125
  108.9 12.1 %all-to-all-done.4 = bf16[4,64,256]{2,1,0:T(8,128)(2,1)S(1)} async-done(((bf16[4,64,256]{2,1,0:T(8,128)(2,1)}), bf16[4,64,256]{2,1,0:T(8,128)(2,1)S(1)}, u32[]{:S(2)}, u32[]{:S(2)}) %all-to-all-start.4) | async-done | bytes 131104 | tf_op jit(solution)/shard_map/all_to_all | solution.py:125
  121.9 4.0 %all-to-all-start.5 = ((bf16[8,64,256]{2,1,0:T(8,128)(2,1)}), bf16[8,64,256]{2,1,0:T(8,128)(2,1)S(1)}, u32[]{:S(2)}, u32[]{:S(2)}) async-start(bf16[8,64,256]{2,1,0:T(8,128)(2,1)} %pad_maximum_fusion), calls=%async_computation.5 | async-start | bytes 524288 | tf_op jit(solution)/shard_map/all_to_all | solution.py:125
  125.9 0.8 fusion
  126.7 9.7 %all-to-all-done.5 = bf16[8,64,256]{2,1,0:T(8,128)(2,1)S(1)} async-done(((bf16[8,64,256]{2,1,0:T(8,128)(2,1)}), bf16[8,64,256]{2,1,0:T(8,128)(2,1)S(1)}, u32[]{:S(2)}, u32[]{:S(2)}) %all-to-all-start.5) | async-done | bytes 262176 | tf_op jit(solution)/shard_map/all_to_all | solution.py:125
  137.1 0.8 convolution_convert_fusion.1
  (46 shorter events, 6.2 us)
Async XLA Ops:
  0.6 125.3 %copy-start = (bf16[256,256]{1,0:T(8,128)(2,1)S(1)}, bf16[256,256]{1,0:T(8,128)(2,1)}, u32[]{:S(2)}) copy-start(bf16[256,256]{1,0:T(8,128)(2,1)} %param.9) | copy-start | bytes 393220
  2.3 39.2 %all-to-all-start = ((bf16[24,32,256]{2,1,0:T(8,128)(2,1)}), bf16[24,32,256]{2,1,0:T(8,128)(2,1)S(1)}, u32[]{:S(2)}, u32[]{:S(2)}) async-start(bf16[24,32,256]{2,1,0:T(8,128)(2,1)} %scale_copies.1), calls=%async_computation | async-start | bytes 786432 | tf_op jit(solution)/shard_map/all_to_all | solution.py:125
  14.8 26.3 %collective-permute-start = (bf16[32,256]{1,0:T(8,128)(2,1)S(1)}, bf16[32,256]{1,0:T(8,128)(2,1)S(1)}, u32[]{:S(2)}, u32[]{:S(2)}) collective-permute-start(bf16[32,256]{1,0:T(8,128)(2,1)S(1)} %get-tuple-element.26), channel_id=1, source_target_pairs={{0,192},{192,384},{384,576},{576,0},{1,193},{193,385},{385,577},{5... | collective-permute-start | bytes 49160 | tf_op jit(solution)/shard_map/ppermute | solution.py:134
  23.9 17.2 %collective-permute-start.1 = (bf16[32,256]{1,0:T(8,128)(2,1)S(1)}, bf16[32,256]{1,0:T(8,128)(2,1)S(1)}, u32[]{:S(2)}, u32[]{:S(2)}) collective-permute-start(bf16[32,256]{1,0:T(8,128)(2,1)S(1)} %get-tuple-element.26), channel_id=1, source_target_pairs={{0,384},{192,576},{384,0},{576,192},{1,385},{193,577},{385,1},{577... | collective-permute-start | bytes 49160 | tf_op jit(solution)/shard_map/ppermute | solution.py:134
  33.9 7.5 %collective-permute-start.2 = (bf16[32,256]{1,0:T(8,128)(2,1)S(1)}, bf16[32,256]{1,0:T(8,128)(2,1)S(1)}, u32[]{:S(2)}, u32[]{:S(2)}) collective-permute-start(bf16[32,256]{1,0:T(8,128)(2,1)S(1)} %get-tuple-element.26), channel_id=1, source_target_pairs={{0,576},{192,0},{384,192},{576,384},{1,577},{193,1},{385,193},{577... | collective-permute-start | bytes 49160 | tf_op jit(solution)/shard_map/ppermute | solution.py:134
  37.6 1.7 %copy-start.1 = (s32[1,1,36,128,128]{4,3,2,1,0:T(8,128)S(1)}, s32[1,1,36,128,128]{4,3,2,1,0:T(8,128)}, u32[]{:S(2)}) copy-start(s32[1,1,36,128,128]{4,3,2,1,0:T(8,128)} %param.12) | copy-start | bytes 7077892
  39.3 0.7 copy-start.2
  42.7 22.1 %all-to-all-start.1 = ((bf16[4,768,256]{2,1,0:T(8,128)(2,1)}), bf16[4,768,256]{2,1,0:T(8,128)(2,1)S(1)}, u32[]{:S(2)}, u32[]{:S(2)}) async-start(bf16[4,768,256]{2,1,0:T(8,128)(2,1)} %broadcast_in_dim.64), calls=%async_computation.1 | async-start | bytes 3145728 | tf_op jit(solution)/shard_map/all_to_all | solution.py:121
  47.4 3.1 %collective-permute-start.3 = (bf16[4,32,256]{2,1,0:T(8,128)(2,1)S(1)}, bf16[4,32,256]{2,1,0:T(8,128)(2,1)S(1)}, u32[]{:S(2)}, u32[]{:S(2)}) collective-permute-start(bf16[4,32,256]{2,1,0:T(8,128)(2,1)S(1)} %bitcast_dynamic-update-slice_fusion.2), channel_id=1, source_target_pairs={{0,96},{96,0},{1,97},{97,1},{2,98},{98,2},{3,99},{99,3},{4,100},{1... | collective-permute-start | bytes 196616 | tf_op jit(solution)/shard_map/ppermute | solution.py:134
  51.2 5.4 %copy-start.3 = (bf16[3072,256]{1,0:T(8,128)(2,1)}, bf16[3072,256]{1,0:T(8,128)(2,1)S(1)}, u32[]{:S(2)}) copy-start(bf16[3072,256]{1,0:T(8,128)(2,1)S(1)} %convolution_convert_fusion) | copy-start | bytes 4718596
  52.4 31.5 %collective-permute-start.4 = (bf16[32,32,256]{2,1,0:T(8,128)(2,1)}, bf16[32,32,256]{2,1,0:T(8,128)(2,1)}, u32[]{:S(2)}, u32[]{:S(2)}) collective-permute-start(bf16[32,32,256]{2,1,0:T(8,128)(2,1)} %get-tuple-element.28), channel_id=1, source_target_pairs={{0,1},{1,2},{2,0},{3,4},{4,5},{5,3},{6,7},{7,8},{8,6},{9,10},{10,1... | collective-permute-start | bytes 1572872 | tf_op jit(solution)/shard_map/ppermute | solution.py:134
  56.6 27.2 %collective-permute-start.5 = (bf16[32,32,256]{2,1,0:T(8,128)(2,1)}, bf16[32,32,256]{2,1,0:T(8,128)(2,1)}, u32[]{:S(2)}, u32[]{:S(2)}) collective-permute-start(bf16[32,32,256]{2,1,0:T(8,128)(2,1)} %get-tuple-element.27), channel_id=1, source_target_pairs={{0,2},{1,0},{2,1},{3,5},{4,3},{5,4},{6,8},{7,6},{8,7},{9,11},{10,9... | collective-permute-start | bytes 1572872 | tf_op jit(solution)/shard_map/ppermute | solution.py:134
  66.3 17.4 %all-to-all-start.2 = ((bf16[16,32,256]{2,1,0:T(8,128)(2,1)}), bf16[16,32,256]{2,1,0:T(8,128)(2,1)S(1)}, u32[]{:S(2)}, u32[]{:S(2)}) async-start(bf16[16,32,256]{2,1,0:T(8,128)(2,1)} %bitcast.14), calls=%async_computation.2 | async-start | bytes 524288 | tf_op jit(solution)/shard_map/all_to_all | solution.py:125
  73.4 3.2 %collective-permute-start.6 = (bf16[4,32,256]{2,1,0:T(8,128)(2,1)S(1)}, bf16[4,32,256]{2,1,0:T(8,128)(2,1)S(1)}, u32[]{:S(2)}, u32[]{:S(2)}) collective-permute-start(bf16[4,32,256]{2,1,0:T(8,128)(2,1)S(1)} %dynamic-slice_bitcast_fusion.5), channel_id=1, source_target_pairs={{0,96},{96,0},{1,97},{97,1},{2,98},{98,2},{3,99},{99,3},{4,100},{1... | collective-permute-start | bytes 196616 | tf_op jit(solution)/shard_map/ppermute | solution.py:134
  84.5 19.7 %all-to-all-start.3 = ((bf16[12,32,256]{2,1,0:T(8,128)(2,1)}), bf16[12,32,256]{2,1,0:T(8,128)(2,1)S(1)}, u32[]{:S(2)}, u32[]{:S(2)}) async-start(bf16[12,32,256]{2,1,0:T(8,128)(2,1)} %broadcast_in_dim.70), calls=%async_computation.3 | async-start | bytes 393216 | tf_op jit(solution)/shard_map/all_to_all | solution.py:121
  93.8 32.1 %copy-start.4 = (s32[32]{0:T(128)S(1)}, s32[32]{0:T(128)}, u32[]{:S(2)}) copy-start(s32[32]{0:T(128)} %param.10) | copy-start | bytes 388
  93.8 10.5 %collective-permute-start.7 = (bf16[8,32,256]{2,1,0:T(8,128)(2,1)S(1)}, bf16[8,32,256]{2,1,0:T(8,128)(2,1)S(1)}, u32[]{:S(2)}, u32[]{:S(2)}) collective-permute-start(bf16[8,32,256]{2,1,0:T(8,128)(2,1)S(1)} %get-tuple-element.31), channel_id=1, source_target_pairs={{0,48},{24,72},{48,0},{72,24},{1,49},{25,73},{49,1},{73,25},{2,50}... | collective-permute-start | bytes 393224 | tf_op jit(solution)/shard_map/ppermute | solution.py:134
  97.2 11.7 %collective-permute-start.9 = (bf16[8,32,256]{2,1,0:T(8,128)(2,1)S(1)}, bf16[8,32,256]{2,1,0:T(8,128)(2,1)S(1)}, u32[]{:S(2)}, u32[]{:S(2)}) collective-permute-start(bf16[8,32,256]{2,1,0:T(8,128)(2,1)S(1)} %get-tuple-element.30), channel_id=1, source_target_pairs={{0,72},{24,0},{48,24},{72,48},{1,73},{25,1},{49,25},{73,49},{2,74}... | collective-permute-start | bytes 393224 | tf_op jit(solution)/shard_map/ppermute | solution.py:134
  99.1 9.7 %collective-permute-start.8 = (bf16[8,32,256]{2,1,0:T(8,128)(2,1)S(1)}, bf16[8,32,256]{2,1,0:T(8,128)(2,1)S(1)}, u32[]{:S(2)}, u32[]{:S(2)}) collective-permute-start(bf16[8,32,256]{2,1,0:T(8,128)(2,1)S(1)} %get-tuple-element.29), channel_id=1, source_target_pairs={{0,24},{24,48},{48,72},{72,0},{1,25},{25,49},{49,73},{73,1},{2,26}... | collective-permute-start | bytes 393224 | tf_op jit(solution)/shard_map/ppermute | solution.py:134
  105.0 16.1 %all-to-all-start.4 = ((bf16[4,64,256]{2,1,0:T(8,128)(2,1)}), bf16[4,64,256]{2,1,0:T(8,128)(2,1)S(1)}, u32[]{:S(2)}, u32[]{:S(2)}) async-start(bf16[4,64,256]{2,1,0:T(8,128)(2,1)} %pad_maximum_fusion.1), calls=%async_computation.4 | async-start | bytes 262144 | tf_op jit(solution)/shard_map/all_to_all | solution.py:125
  121.9 14.5 %all-to-all-start.5 = ((bf16[8,64,256]{2,1,0:T(8,128)(2,1)}), bf16[8,64,256]{2,1,0:T(8,128)(2,1)S(1)}, u32[]{:S(2)}, u32[]{:S(2)}) async-start(bf16[8,64,256]{2,1,0:T(8,128)(2,1)} %pad_maximum_fusion), calls=%async_computation.5 | async-start | bytes 524288 | tf_op jit(solution)/shard_map/all_to_all | solution.py:125

commit v3 on v2

--- a/solution.py
+++ b/solution.py
@@ -181,22 +181,21 @@
     backward = lax.dot_general(
         dense, targets, (((0,), (0,)), ((), ())), preferred_element_type=f32
     ).astype(bf16)
-    thirds = backward.reshape(-1, SIZES["zl"], mine, width)
-    kept, second, third = (block_of(thirds, "zl", step, 1) for step in range(3))
-    second, third = shifted(second, "zl", 1), shifted(third, "zl", 2)
+    quarters = backward.reshape(SIZES["x"], -1, width)
+    kept, *sent = (block_of(quarters, "x", step, 0) for step in range(4))
+    sent = [shifted(block, "x", step + 1) for step, block in enumerate(sent)]
 
     forward, outer = dense_products(dense, sources, targets)
-    outer = copies_of(outer.reshape(SIZES["y"], -1, width), ("core",))
-    outer = total(swap(outer.reshape(-1, *outer.shape[2:]), ("core", "y"))).astype(bf16)
+    outer = swap(outer.reshape(SIZES["y"], -1, width), ("y",))
+    outer = total(outer).astype(bf16)
     forward = forward.reshape(SIZES["zh"], SIZES["core"], mine, width)
     other = shifted(block_of(forward, "core", 1, 1), "core", 1)
     forward = sum_of((block_of(forward, "core", 0, 1), other))
-    outer, second, third, forward = lax.optimization_barrier((outer, second, third, forward))
-    part = sum_of((kept, second, third)).reshape(SIZES["x"], -1, mine, width)
-    kept, first, second, third = (block_of(part, "x", step, 0) for step in range(4))
-    outer = total(spread(outer, ("x", "zl"))).astype(bf16)
-    outer, second = lax.optimization_barrier((outer, shifted(second, "x", 2)))
-    part = sum_of((kept, shifted(first, "x", 1), second, shifted(third, "x", 3)))
+    outer, sent = lax.optimization_barrier((outer, sent))
+    part = sum_of([kept, *sent]).reshape(SIZES["y"], SIZES["zl"], mine, width)
+    kept, second, third = (block_of(part, "zl", step, 1) for step in range(3))
+    outer = total(spread(outer, ("core", "x", "zl"))).astype(bf16)
+    part = sum_of((kept, shifted(second, "zl", 1), shifted(third, "zl", 2)))
     both = total(swap(beside(forward, outer), ("zh",)))
     forward_mine, outer = both[:mine], both[mine:].astype(bf16)
     output = (

time: 139 us -> 140 us (level)
  blocking collectives: 0 us -> 15.9 us
  starting transfers between devices: 82.9 us -> 73.1 us
  waiting for transfers between devices: 35.9 us -> 31 us
    all_to_all x0 -> x1, blocking collectives: none -> 15.9 us  [swap(): return lax.all_to_all(pieces, axes, 0, 0)]
    all_to_all x4 -> x3, waiting for transfers between devices: 29 us -> 20.9 us  [swap(): return lax.all_to_all(pieces, axes, 0, 0)]
    all_to_all x4 -> x3, starting transfers between devices: 25.8 us -> 19.7 us  [swap(): return lax.all_to_all(pieces, axes, 0, 0)]
    ppermute x10, starting transfers between devices: 44.8 us -> 41 us  [shifted(): lax.ppermute(piece, axis, [(i, (i + step) % size) for i in range(size)])]
    all_to_all x2, waiting for transfers between devices: 4.45 us -> 6.57 us  [spread(): return lax.all_to_all(copies_of(piece, axes), axes, 0, 0)]
  transfers between devices with their start and end apart: 16 -> 15, of which waited for: 7 -> 7; matrix products, arithmetic and copies ran while one was open for 5% -> 5% of each run, Pallas kernels for 1% -> 1%
where the time goes in v3:
time: 140 us; the launch traced here: 139 us
  starting transfers between devices  73.1 us (52%)
  waiting for transfers between devices  31 us (22%)
  blocking collectives  15.9 us (11%)
  local copies, waits for them, and re-layouts  5.67 us (4%)
  other arithmetic  5.35 us (4%)
  Pallas kernels  3.58 us (3%)
  matrix products  2.18 us (2%)
  between operations  1.76 us (1%)
    ppermute x10, starting transfers between devices, shifted(): lax.ppermute(piece, axis, [(i, (i + step) % size) for i in range(size)])  41 us
    all_to_all x3, waiting for transfers between devices, swap(): return lax.all_to_all(pieces, axes, 0, 0)  20.9 us
    all_to_all x3, starting transfers between devices, swap(): return lax.all_to_all(pieces, axes, 0, 0)  19.7 us
    all_to_all x1, blocking collectives, swap(): return lax.all_to_all(pieces, axes, 0, 0)  15.9 us
    all_to_all x2, starting transfers between devices, spread(): return lax.all_to_all(copies_of(piece, axes), axes, 0, 0)  12.4 us
    all_to_all x2, waiting for transfers between devices, spread(): return lax.all_to_all(copies_of(piece, axes), axes, 0, 0)  6.57 us
    ppermute x10, waiting for transfers between devices, shifted(): lax.ppermute(piece, axis, [(i, (i + step) % size) for i in range(size)])  3.53 us
  transfers between devices with their start and end apart: 15, of which 7 were waited for; matrix products, arithmetic and copies ran while one was open for 5% of the time, Pallas kernels for 1%

profile of v3, /device:TPU:6, one launch (start us, length us, event | category | flops | bytes accessed | tf_op | source)
XLA Modules:
  0.0 138.5 jit_solution(7596119337619741263)
XLA Ops:
  0.6 1.7 %scale_copies.1 = bf16[24,32,256]{2,1,0:T(8,128)(2,1)} custom-call(s32[1,32]{1,0:T(1,128)} %bitcast.67, bf16[32,256]{1,0:T(8,128)(2,1)} %value_ref.1), custom_call_target="tpu_custom_call" | custom-call | tf_op jit(solution)/shard_map/scale_copies/pallas_call | solution.py:48
  2.3 11.0 %all-to-all-start = ((bf16[24,32,256]{2,1,0:T(8,128)(2,1)}), bf16[24,32,256]{2,1,0:T(8,128)(2,1)S(1)}, u32[]{:S(2)}, u32[]{:S(2)}) async-start(bf16[24,32,256]{2,1,0:T(8,128)(2,1)} %scale_copies.1), calls=%async_computation | async-start | bytes 786432 | tf_op jit(solution)/shard_map/all_to_all | solution.py:125
  14.0 0.8 bitcast_dynamic-update-slice_fusion.5
  14.8 9.1 %collective-permute-start = (bf16[32,256]{1,0:T(8,128)(2,1)S(1)}, bf16[32,256]{1,0:T(8,128)(2,1)S(1)}, u32[]{:S(2)}, u32[]{:S(2)}) collective-permute-start(bf16[32,256]{1,0:T(8,128)(2,1)S(1)} %get-tuple-element.22), channel_id=1, source_target_pairs={{0,192},{192,384},{384,576},{576,0},{1,193},{193,385},{385,577},{5... | collective-permute-start | bytes 49160 | tf_op jit(solution)/shard_map/ppermute | solution.py:134
  23.9 10.0 %collective-permute-start.1 = (bf16[32,256]{1,0:T(8,128)(2,1)S(1)}, bf16[32,256]{1,0:T(8,128)(2,1)S(1)}, u32[]{:S(2)}, u32[]{:S(2)}) collective-permute-start(bf16[32,256]{1,0:T(8,128)(2,1)S(1)} %get-tuple-element.22), channel_id=1, source_target_pairs={{0,384},{192,576},{384,0},{576,192},{1,385},{193,577},{385,1},{577... | collective-permute-start | bytes 49160 | tf_op jit(solution)/shard_map/ppermute | solution.py:134
  33.9 3.0 %collective-permute-start.2 = (bf16[32,256]{1,0:T(8,128)(2,1)S(1)}, bf16[32,256]{1,0:T(8,128)(2,1)S(1)}, u32[]{:S(2)}, u32[]{:S(2)}) collective-permute-start(bf16[32,256]{1,0:T(8,128)(2,1)S(1)} %get-tuple-element.22), channel_id=1, source_target_pairs={{0,576},{192,0},{384,192},{576,384},{1,577},{193,1},{385,193},{577... | collective-permute-start | bytes 49160 | tf_op jit(solution)/shard_map/ppermute | solution.py:134
  37.7 1.7 %copy-done.1 = s32[1,1,36,128,128]{4,3,2,1,0:T(8,128)S(1)} copy-done((s32[1,1,36,128,128]{4,3,2,1,0:T(8,128)S(1)}, s32[1,1,36,128,128]{4,3,2,1,0:T(8,128)}, u32[]{:S(2)}) %copy-start.1) | copy-done | bytes 2359320
  40.0 1.1 place_tiles.1.dense_ref
  41.4 1.2 broadcast_in_dim.57
  42.7 4.8 %all-to-all-start.1 = ((bf16[4,768,256]{2,1,0:T(8,128)(2,1)}), bf16[4,768,256]{2,1,0:T(8,128)(2,1)S(1)}, u32[]{:S(2)}, u32[]{:S(2)}) async-start(bf16[4,768,256]{2,1,0:T(8,128)(2,1)} %broadcast_in_dim.57), calls=%async_computation.1 | async-start | bytes 3145728 | tf_op jit(solution)/shard_map/all_to_all | solution.py:121
  47.5 1.9 %collective-permute-start.3 = (bf16[4,32,256]{2,1,0:T(8,128)(2,1)S(1)}, bf16[4,32,256]{2,1,0:T(8,128)(2,1)S(1)}, u32[]{:S(2)}, u32[]{:S(2)}) collective-permute-start(bf16[4,32,256]{2,1,0:T(8,128)(2,1)S(1)} %bitcast_dynamic-update-slice_fusion.2), channel_id=1, source_target_pairs={{0,96},{96,0},{1,97},{97,1},{2,98},{98,2},{3,99},{99,3},{4,100},{1... | collective-permute-start | bytes 196616 | tf_op jit(solution)/shard_map/ppermute | solution.py:134
  49.4 1.2 collective-permute-done.3
  51.3 1.2 dynamic-slice_bitcast_fusion
  52.4 1.9 %collective-permute-start.5 = (bf16[768,256]{1,0:T(8,128)(2,1)}, bf16[768,256]{1,0:T(8,128)(2,1)}, u32[]{:S(2)}, u32[]{:S(2)}) collective-permute-start(bf16[768,256]{1,0:T(8,128)(2,1)} %get-tuple-element.25), channel_id=1, source_target_pairs={{0,24},{24,48},{48,72},{72,0},{1,25},{25,49},{49,73},{73,1},{2,26}... | collective-permute-start | bytes 1179656 | tf_op jit(solution)/shard_map/ppermute | solution.py:134
  54.3 4.8 %collective-permute-start.6 = (bf16[768,256]{1,0:T(8,128)(2,1)}, bf16[768,256]{1,0:T(8,128)(2,1)}, u32[]{:S(2)}, u32[]{:S(2)}) collective-permute-start(bf16[768,256]{1,0:T(8,128)(2,1)} %get-tuple-element.24), channel_id=1, source_target_pairs={{0,48},{24,72},{48,0},{72,24},{1,49},{25,73},{49,1},{73,25},{2,50}... | collective-permute-start | bytes 1179656 | tf_op jit(solution)/shard_map/ppermute | solution.py:134
  59.2 1.9 %collective-permute-start.7 = (bf16[768,256]{1,0:T(8,128)(2,1)}, bf16[768,256]{1,0:T(8,128)(2,1)}, u32[]{:S(2)}, u32[]{:S(2)}) collective-permute-start(bf16[768,256]{1,0:T(8,128)(2,1)} %get-tuple-element.23), channel_id=1, source_target_pairs={{0,72},{24,0},{48,24},{72,48},{1,73},{25,1},{49,25},{73,49},{2,74}... | collective-permute-start | bytes 1179656 | tf_op jit(solution)/shard_map/ppermute | solution.py:134
  61.1 6.6 %all-to-all-done.1.source_ref = bf16[4,768,256]{2,1,0:T(8,128)(2,1)S(1)} async-done(((bf16[4,768,256]{2,1,0:T(8,128)(2,1)}), bf16[4,768,256]{2,1,0:T(8,128)(2,1)S(1)}, u32[]{:S(2)}, u32[]{:S(2)}) %all-to-all-start.1) | async-done | bytes 1572896 | tf_op jit(solution)/shard_map/all_to_all | solution.py:121
  67.7 0.8 apply_dense.1
  68.5 15.9 %all_to_all.30 = bf16[8,32,256]{2,1,0:T(8,128)(2,1)S(1)} all-to-all(bf16[8,32,256]{2,1,0:T(8,128)(2,1)S(1)} %bitcast.60), channel_id=1, replica_groups=mesh['zh'=4,'core'=2,'x'=4,'y'=8,'zl'=3] {'y'}, dimensions={0} | all-to-all | bytes 262144 | tf_op jit(solution)/shard_map/all_to_all | solution.py:125
  84.5 0.8 broadcast_in_dim.61
  85.3 7.7 %all-to-all-start.3 = ((bf16[24,32,256]{2,1,0:T(8,128)(2,1)}), bf16[24,32,256]{2,1,0:T(8,128)(2,1)S(1)}, u32[]{:S(2)}, u32[]{:S(2)}) async-start(bf16[24,32,256]{2,1,0:T(8,128)(2,1)} %broadcast_in_dim.61), calls=%async_computation.3 | async-start | bytes 786432 | tf_op jit(solution)/shard_map/all_to_all | solution.py:121
  93.0 2.1 %collective-permute-start.4 = (bf16[4,32,256]{2,1,0:T(8,128)(2,1)S(1)}, bf16[4,32,256]{2,1,0:T(8,128)(2,1)S(1)}, u32[]{:S(2)}, u32[]{:S(2)}) collective-permute-start(bf16[4,32,256]{2,1,0:T(8,128)(2,1)S(1)} %dynamic-slice_bitcast_fusion.5), channel_id=1, source_target_pairs={{0,96},{96,0},{1,97},{97,1},{2,98},{98,2},{3,99},{99,3},{4,100},{1... | collective-permute-start | bytes 196616 | tf_op jit(solution)/shard_map/ppermute | solution.py:134
  95.2 1.0 collective-permute-done.4
  96.2 1.6 %fusion.3 = bf16[768,256]{1,0:T(8,128)(2,1)S(1)} fusion(bf16[768,256]{1,0:T(8,128)(2,1)} %collective-permute-done.7, bf16[768,256]{1,0:T(8,128)(2,1)} %collective-permute-done.6, bf16[768,256]{1,0:T(8,128)(2,1)} %collective-permute-done.5, bf16[4,768,256]{2,1,0:T(8,128)(2,1)} %bitcast.63, s32[]{:T(128)S(6)} %select_n.130), kind=kLoop, calls=%fused_computation.7 | loop fusion | flops 1572864 | bytes 1966084 | tf_op jit(solution)/shard_map/convert_element_type | solution.py:155
  97.8 4.3 %collective-permute-start.9 = (bf16[8,32,256]{2,1,0:T(8,128)(2,1)S(1)}, bf16[8,32,256]{2,1,0:T(8,128)(2,1)S(1)}, u32[]{:S(2)}, u32[]{:S(2)}) collective-permute-start(bf16[8,32,256]{2,1,0:T(8,128)(2,1)S(1)} %get-tuple-element.27), channel_id=1, source_target_pairs={{0,2},{1,0},{2,1},{3,5},{4,3},{5,4},{6,8},{7,6},{8,7},{9,11},{10,9... | collective-permute-start | bytes 393224 | tf_op jit(solution)/shard_map/ppermute | solution.py:134
  102.1 1.9 %collective-permute-start.8 = (bf16[8,32,256]{2,1,0:T(8,128)(2,1)S(1)}, bf16[8,32,256]{2,1,0:T(8,128)(2,1)S(1)}, u32[]{:S(2)}, u32[]{:S(2)}) collective-permute-start(bf16[8,32,256]{2,1,0:T(8,128)(2,1)S(1)} %get-tuple-element.26), channel_id=1, source_target_pairs={{0,1},{1,2},{2,0},{3,4},{4,5},{5,3},{6,7},{7,8},{8,6},{9,10},{10,1... | collective-permute-start | bytes 393224 | tf_op jit(solution)/shard_map/ppermute | solution.py:134
  104.8 4.4 %all-to-all-start.4 = ((bf16[4,64,256]{2,1,0:T(8,128)(2,1)}), bf16[4,64,256]{2,1,0:T(8,128)(2,1)S(1)}, u32[]{:S(2)}, u32[]{:S(2)}) async-start(bf16[4,64,256]{2,1,0:T(8,128)(2,1)} %pad_maximum_fusion.1), calls=%async_computation.4 | async-start | bytes 262144 | tf_op jit(solution)/shard_map/all_to_all | solution.py:125
  109.1 1.0 collective-permute-done.8
  110.2 11.2 %all-to-all-done.4 = bf16[4,64,256]{2,1,0:T(8,128)(2,1)S(1)} async-done(((bf16[4,64,256]{2,1,0:T(8,128)(2,1)}), bf16[4,64,256]{2,1,0:T(8,128)(2,1)S(1)}, u32[]{:S(2)}, u32[]{:S(2)}) %all-to-all-start.4) | async-done | bytes 131104 | tf_op jit(solution)/shard_map/all_to_all | solution.py:125
  122.2 4.3 %all-to-all-start.5 = ((bf16[8,64,256]{2,1,0:T(8,128)(2,1)}), bf16[8,64,256]{2,1,0:T(8,128)(2,1)S(1)}, u32[]{:S(2)}, u32[]{:S(2)}) async-start(bf16[8,64,256]{2,1,0:T(8,128)(2,1)} %pad_maximum_fusion), calls=%async_computation.5 | async-start | bytes 524288 | tf_op jit(solution)/shard_map/all_to_all | solution.py:125
  127.2 9.7 %all-to-all-done.5 = bf16[8,64,256]{2,1,0:T(8,128)(2,1)S(1)} async-done(((bf16[8,64,256]{2,1,0:T(8,128)(2,1)}), bf16[8,64,256]{2,1,0:T(8,128)(2,1)S(1)}, u32[]{:S(2)}, u32[]{:S(2)}) %all-to-all-start.5) | async-done | bytes 262176 | tf_op jit(solution)/shard_map/all_to_all | solution.py:125
  137.7 0.8 convolution_convert_fusion.1
  (44 shorter events, 5.5 us)
Async XLA Ops:
  0.6 125.9 %copy-start = (bf16[256,256]{1,0:T(8,128)(2,1)S(1)}, bf16[256,256]{1,0:T(8,128)(2,1)}, u32[]{:S(2)}) copy-start(bf16[256,256]{1,0:T(8,128)(2,1)} %param.9) | copy-start | bytes 393220
  2.3 39.2 %all-to-all-start = ((bf16[24,32,256]{2,1,0:T(8,128)(2,1)}), bf16[24,32,256]{2,1,0:T(8,128)(2,1)S(1)}, u32[]{:S(2)}, u32[]{:S(2)}) async-start(bf16[24,32,256]{2,1,0:T(8,128)(2,1)} %scale_copies.1), calls=%async_computation | async-start | bytes 786432 | tf_op jit(solution)/shard_map/all_to_all | solution.py:125
  14.8 26.3 %collective-permute-start = (bf16[32,256]{1,0:T(8,128)(2,1)S(1)}, bf16[32,256]{1,0:T(8,128)(2,1)S(1)}, u32[]{:S(2)}, u32[]{:S(2)}) collective-permute-start(bf16[32,256]{1,0:T(8,128)(2,1)S(1)} %get-tuple-element.22), channel_id=1, source_target_pairs={{0,192},{192,384},{384,576},{576,0},{1,193},{193,385},{385,577},{5... | collective-permute-start | bytes 49160 | tf_op jit(solution)/shard_map/ppermute | solution.py:134
  23.9 17.2 %collective-permute-start.1 = (bf16[32,256]{1,0:T(8,128)(2,1)S(1)}, bf16[32,256]{1,0:T(8,128)(2,1)S(1)}, u32[]{:S(2)}, u32[]{:S(2)}) collective-permute-start(bf16[32,256]{1,0:T(8,128)(2,1)S(1)} %get-tuple-element.22), channel_id=1, source_target_pairs={{0,384},{192,576},{384,0},{576,192},{1,385},{193,577},{385,1},{577... | collective-permute-start | bytes 49160 | tf_op jit(solution)/shard_map/ppermute | solution.py:134
  33.9 7.5 %collective-permute-start.2 = (bf16[32,256]{1,0:T(8,128)(2,1)S(1)}, bf16[32,256]{1,0:T(8,128)(2,1)S(1)}, u32[]{:S(2)}, u32[]{:S(2)}) collective-permute-start(bf16[32,256]{1,0:T(8,128)(2,1)S(1)} %get-tuple-element.22), channel_id=1, source_target_pairs={{0,576},{192,0},{384,192},{576,384},{1,577},{193,1},{385,193},{577... | collective-permute-start | bytes 49160 | tf_op jit(solution)/shard_map/ppermute | solution.py:134
  37.7 1.7 %copy-start.1 = (s32[1,1,36,128,128]{4,3,2,1,0:T(8,128)S(1)}, s32[1,1,36,128,128]{4,3,2,1,0:T(8,128)}, u32[]{:S(2)}) copy-start(s32[1,1,36,128,128]{4,3,2,1,0:T(8,128)} %param.12) | copy-start | bytes 7077892
  39.3 0.7 copy-start.2
  42.7 25.0 %all-to-all-start.1 = ((bf16[4,768,256]{2,1,0:T(8,128)(2,1)}), bf16[4,768,256]{2,1,0:T(8,128)(2,1)S(1)}, u32[]{:S(2)}, u32[]{:S(2)}) async-start(bf16[4,768,256]{2,1,0:T(8,128)(2,1)} %broadcast_in_dim.57), calls=%async_computation.1 | async-start | bytes 3145728 | tf_op jit(solution)/shard_map/all_to_all | solution.py:121
  47.5 3.1 %collective-permute-start.3 = (bf16[4,32,256]{2,1,0:T(8,128)(2,1)S(1)}, bf16[4,32,256]{2,1,0:T(8,128)(2,1)S(1)}, u32[]{:S(2)}, u32[]{:S(2)}) collective-permute-start(bf16[4,32,256]{2,1,0:T(8,128)(2,1)S(1)} %bitcast_dynamic-update-slice_fusion.2), channel_id=1, source_target_pairs={{0,96},{96,0},{1,97},{97,1},{2,98},{98,2},{3,99},{99,3},{4,100},{1... | collective-permute-start | bytes 196616 | tf_op jit(solution)/shard_map/ppermute | solution.py:134
  51.2 7.9 %copy-start.3 = (bf16[3072,256]{1,0:T(8,128)(2,1)}, bf16[3072,256]{1,0:T(8,128)(2,1)S(1)}, u32[]{:S(2)}) copy-start(bf16[3072,256]{1,0:T(8,128)(2,1)S(1)} %convolution_convert_fusion) | copy-start | bytes 4718596
  52.4 32.1 %collective-permute-start.5 = (bf16[768,256]{1,0:T(8,128)(2,1)}, bf16[768,256]{1,0:T(8,128)(2,1)}, u32[]{:S(2)}, u32[]{:S(2)}) collective-permute-start(bf16[768,256]{1,0:T(8,128)(2,1)} %get-tuple-element.25), channel_id=1, source_target_pairs={{0,24},{24,48},{48,72},{72,0},{1,25},{25,49},{49,73},{73,1},{2,26}... | collective-permute-start | bytes 1179656 | tf_op jit(solution)/shard_map/ppermute | solution.py:134
  54.3 30.1 %collective-permute-start.6 = (bf16[768,256]{1,0:T(8,128)(2,1)}, bf16[768,256]{1,0:T(8,128)(2,1)}, u32[]{:S(2)}, u32[]{:S(2)}) collective-permute-start(bf16[768,256]{1,0:T(8,128)(2,1)} %get-tuple-element.24), channel_id=1, source_target_pairs={{0,48},{24,72},{48,0},{72,24},{1,49},{25,73},{49,1},{73,25},{2,50}... | collective-permute-start | bytes 1179656 | tf_op jit(solution)/shard_map/ppermute | solution.py:134
  59.2 25.3 %collective-permute-start.7 = (bf16[768,256]{1,0:T(8,128)(2,1)}, bf16[768,256]{1,0:T(8,128)(2,1)}, u32[]{:S(2)}, u32[]{:S(2)}) collective-permute-start(bf16[768,256]{1,0:T(8,128)(2,1)} %get-tuple-element.23), channel_id=1, source_target_pairs={{0,72},{24,0},{48,24},{72,48},{1,73},{25,1},{49,25},{73,49},{2,74}... | collective-permute-start | bytes 1179656 | tf_op jit(solution)/shard_map/ppermute | solution.py:134
  85.3 18.7 %all-to-all-start.3 = ((bf16[24,32,256]{2,1,0:T(8,128)(2,1)}), bf16[24,32,256]{2,1,0:T(8,128)(2,1)S(1)}, u32[]{:S(2)}, u32[]{:S(2)}) async-start(bf16[24,32,256]{2,1,0:T(8,128)(2,1)} %broadcast_in_dim.61), calls=%async_computation.3 | async-start | bytes 786432 | tf_op jit(solution)/shard_map/all_to_all | solution.py:121
  93.0 3.1 %collective-permute-start.4 = (bf16[4,32,256]{2,1,0:T(8,128)(2,1)S(1)}, bf16[4,32,256]{2,1,0:T(8,128)(2,1)S(1)}, u32[]{:S(2)}, u32[]{:S(2)}) collective-permute-start(bf16[4,32,256]{2,1,0:T(8,128)(2,1)S(1)} %dynamic-slice_bitcast_fusion.5), channel_id=1, source_target_pairs={{0,96},{96,0},{1,97},{97,1},{2,98},{98,2},{3,99},{99,3},{4,100},{1... | collective-permute-start | bytes 196616 | tf_op jit(solution)/shard_map/ppermute | solution.py:134
  97.8 28.7 %copy-start.4 = (s32[32]{0:T(128)S(1)}, s32[32]{0:T(128)}, u32[]{:S(2)}) copy-start(s32[32]{0:T(128)} %param.10) | copy-start | bytes 388
  97.8 11.3 %collective-permute-start.9 = (bf16[8,32,256]{2,1,0:T(8,128)(2,1)S(1)}, bf16[8,32,256]{2,1,0:T(8,128)(2,1)S(1)}, u32[]{:S(2)}, u32[]{:S(2)}) collective-permute-start(bf16[8,32,256]{2,1,0:T(8,128)(2,1)S(1)} %get-tuple-element.27), channel_id=1, source_target_pairs={{0,2},{1,0},{2,1},{3,5},{4,3},{5,4},{6,8},{7,6},{8,7},{9,11},{10,9... | collective-permute-start | bytes 393224 | tf_op jit(solution)/shard_map/ppermute | solution.py:134
  102.1 8.1 %collective-permute-start.8 = (bf16[8,32,256]{2,1,0:T(8,128)(2,1)S(1)}, bf16[8,32,256]{2,1,0:T(8,128)(2,1)S(1)}, u32[]{:S(2)}, u32[]{:S(2)}) collective-permute-start(bf16[8,32,256]{2,1,0:T(8,128)(2,1)S(1)} %get-tuple-element.26), channel_id=1, source_target_pairs={{0,1},{1,2},{2,0},{3,4},{4,5},{5,3},{6,7},{7,8},{8,6},{9,10},{10,1... | collective-permute-start | bytes 393224 | tf_op jit(solution)/shard_map/ppermute | solution.py:134
  104.8 16.6 %all-to-all-start.4 = ((bf16[4,64,256]{2,1,0:T(8,128)(2,1)}), bf16[4,64,256]{2,1,0:T(8,128)(2,1)S(1)}, u32[]{:S(2)}, u32[]{:S(2)}) async-start(bf16[4,64,256]{2,1,0:T(8,128)(2,1)} %pad_maximum_fusion.1), calls=%async_computation.4 | async-start | bytes 262144 | tf_op jit(solution)/shard_map/all_to_all | solution.py:125
  122.2 14.8 %all-to-all-start.5 = ((bf16[8,64,256]{2,1,0:T(8,128)(2,1)}), bf16[8,64,256]{2,1,0:T(8,128)(2,1)S(1)}, u32[]{:S(2)}, u32[]{:S(2)}) async-start(bf16[8,64,256]{2,1,0:T(8,128)(2,1)} %pad_maximum_fusion), calls=%async_computation.5 | async-start | bytes 524288 | tf_op jit(solution)/shard_map/all_to_all | solution.py:125
